TPU v7x, 32 devices: a whole 2x2x4 slice. The times are simulated.
32 devices in a mesh: segment: 4 (over z), expert: 8 (over y, x, core).
Axes of the slice: x: 2, y: 2, z: 4, core: 2. Of those that a mesh axis runs over, the one named last changes fastest.
Arguments:
- states: bfloat16 [1024, 2048], P('expert'), may hold values from -40 to 40
- cand_len: int32 [16], P('expert'), may hold values from 48 to 64
- routes: int32 [4, 1024, 2], P('segment', 'expert'), may hold values from 0 to 3, as said below
- enc_kv: bfloat16 [4, 32, 2048], P(None, ('segment', 'expert')), may hold values from -900 to 900
- attn_gain: float32 [4, 2048], P('segment'), may hold values from 0.25 to 1.75
- ffn_gain: float32 [4, 2048], P('segment'), may hold values from 0.25 to 1.75
- w_query: bfloat16 [4, 2048, 1024], P('segment'), may hold values from -0.125 to 0.125
- w_out: bfloat16 [4, 1024, 2048], P('segment'), may hold values from -0.1875 to 0.1875
- w_router: bfloat16 [4, 2048, 4], P('segment'), may hold values from -0.125 to 0.125
- w_in: bfloat16 [4, 8, 2048, 2048], P('segment', 'expert'), may hold values from -0.125 to 0.125
- w_down: bfloat16 [4, 8, 2048, 2048], P('segment', 'expert'), may hold values from -0.09375 to 0.09375
Outputs:
- layer_states: bfloat16 [4, 1024, 2048], P('segment', 'expert')
Inputs may be any that keep to these rules, and one draw needn't show every extreme that they name: `routes`: the two experts of a row differ. Within one layer and one candidate, at most 40 rows at positions below that candidate's length name any one expert; in every layer some expert is named by exactly 40 such rows of the first of the 2 candidates of every index of expert.
All inputs are finite; a program needn't handle non-finite values.
Results may differ from a plain program's by a relative error of at most 0.023.
Values may be sent and summed in bfloat16 or wider, within the bound.
No kernel may reach another device: no remote copies, remote signals or barrier semaphores. Data moves between devices by JAX's collectives and lax.ppermute only.
A program may use at most 128 MiB of HBM per device.

v0:
```python
import math

import jax
import jax.numpy as jnp
from jax import lax
from jax.sharding import PartitionSpec as P

HEAD_DIM = 128
CAND_LEN = 64
CAND_DEV = 2


EPSILON = 1e-05


def shifted(shard, axis, by):
    length = lax.axis_size(axis)
    pairs = [(i, i + by) for i in range(length) if 0 <= i + by < length]
    return lax.ppermute(shard, axis, pairs)


def normalize(carried, gain_row):
    average = jnp.mean(carried, axis=-1, keepdims=True)
    centered = carried - average
    variance = jnp.mean(centered * centered, axis=-1, keepdims=True)
    return gain_row * centered * lax.rsqrt(variance + EPSILON)


def route_gates(ffn_input, router, route_block):
    logits = jnp.dot(ffn_input, router, preferred_element_type=jnp.float32)
    labels = jnp.arange(router.shape[1], dtype=jnp.int32)[None, :]
    logit_first = jnp.sum(jnp.where(route_block[:, 0:1] == labels, logits, 0.0), axis=1)
    logit_second = jnp.sum(jnp.where(route_block[:, 1:2] == labels, logits, 0.0), axis=1)
    gate_first = jax.nn.sigmoid(logit_first - logit_second)
    return jnp.stack([gate_first, 1.0 - gate_first], axis=1)


def slot_table(route_block, live_rows, experts, capacity):
    flat_routes = route_block.reshape(-1)
    usable = jnp.repeat(live_rows, 2)
    labels = jnp.arange(experts, dtype=jnp.int32)[None, :]
    onehot = ((flat_routes[:, None] == labels) & usable[:, None]).astype(jnp.int32)
    before = jnp.cumsum(onehot, axis=0) - onehot
    slot_index = jnp.sum(before * onehot, axis=1)
    target = flat_routes * capacity + slot_index
    return (target.reshape(-1, 2), usable.reshape(-1, 2))


def dispatch(ffn_input, target, usable, slot_count):
    labels = jnp.arange(slot_count, dtype=jnp.int32)[:, None]
    select = (labels == target[None, :, 0]) & usable[None, :, 0] | (
        labels == target[None, :, 1]
    ) & usable[None, :, 1]
    return jnp.dot(
        select.astype(jnp.bfloat16), ffn_input, preferred_element_type=jnp.float32
    ).astype(jnp.bfloat16)


def combine(expert_out, target, usable, gate_pair):
    picked = jnp.take(expert_out, jnp.where(usable, target, 0), axis=0).astype(jnp.float32)
    weight = jnp.where(usable, gate_pair, 0.0)
    return jnp.sum(picked * weight[:, :, None], axis=1)


def local(
    states, cand_len, routes, enc_kv, attn_gain, ffn_gain, w_query, w_out, w_router, w_in, w_down
):
    segment_index = lax.axis_index("segment")
    n_segment = lax.axis_size("segment")
    model_width = states.shape[1]
    head_total = w_query.shape[2]
    head_count = head_total // HEAD_DIM
    experts = w_router.shape[2]
    capacity = 2 * ((5 * CAND_LEN + 4 * experts - 1) // (4 * experts))
    score_scale = 1.0 / math.sqrt(HEAD_DIM)
    layer_kv = lax.all_to_all(enc_kv, "segment", split_axis=0, concat_axis=1, tiled=True)
    cached = lax.all_gather(layer_kv, "expert", axis=1, tiled=True)
    key_cache = cached[0, :, :head_total].reshape(-1, head_count, HEAD_DIM)
    value_cache = cached[0, :, head_total:].reshape(-1, head_count, HEAD_DIM)
    inputs = states.reshape(CAND_DEV, CAND_LEN, model_width)
    route_all = routes[0].reshape(CAND_DEV, CAND_LEN, 2)
    position = jnp.arange(CAND_LEN, dtype=jnp.int32)
    outputs = jnp.zeros((CAND_DEV, CAND_LEN, model_width), jnp.bfloat16)
    incoming = jnp.zeros((CAND_LEN, model_width), jnp.bfloat16)
    step_count = CAND_DEV + n_segment - 1
    for step_index in range(step_count):
        micro_step = step_index - segment_index
        active = (micro_step >= 0) & (micro_step < CAND_DEV)
        micro_index = jnp.clip(micro_step, 0, CAND_DEV - 1)
        fresh_rows = inputs[min(step_index, CAND_DEV - 1)]
        current = jnp.where(segment_index == 0, fresh_rows, incoming)
        route_block = lax.dynamic_index_in_dim(route_all, micro_index, 0, keepdims=False)
        length = lax.dynamic_index_in_dim(cand_len, micro_index, 0, keepdims=False)
        row_count = current.shape[0]
        carried = current.astype(jnp.float32)
        normed = normalize(carried, attn_gain[0]).astype(jnp.bfloat16)
        queries = jnp.dot(normed, w_query[0], preferred_element_type=jnp.float32).astype(
            jnp.bfloat16
        )
        query_heads = queries.reshape(row_count, head_count, HEAD_DIM)
        scores = (
            jnp.einsum("tnk,snk->nts", query_heads, key_cache, preferred_element_type=jnp.float32)
            * score_scale
        )
        largest = jnp.max(scores, axis=2, keepdims=True)
        exponent = jnp.exp(scores - largest)
        attn_weights = (exponent / jnp.sum(exponent, axis=2, keepdims=True)).astype(jnp.bfloat16)
        context = jnp.einsum(
            "nts,snk->tnk", attn_weights, value_cache, preferred_element_type=jnp.float32
        )
        context = context.astype(jnp.bfloat16).reshape(row_count, head_total)
        after_attn = carried + jnp.dot(context, w_out[0], preferred_element_type=jnp.float32)
        ffn_input = normalize(after_attn, ffn_gain[0]).astype(jnp.bfloat16)
        gate_pair = route_gates(ffn_input, w_router[0], route_block)
        apply_slot_depth = capacity * (row_count // CAND_LEN)
        target, usable = slot_table(route_block, position < length, experts, apply_slot_depth)
        apply_buffer = dispatch(ffn_input, target, usable, experts * apply_slot_depth)
        outgoing = jnp.repeat(
            apply_buffer.reshape(experts, apply_slot_depth, model_width), 2, axis=0
        )
        received = lax.all_to_all(outgoing, "expert", split_axis=0, concat_axis=0, tiled=True)
        flat_rows = received.reshape(-1, model_width)
        hidden = jnp.maximum(
            jnp.dot(flat_rows, w_in[0, 0], preferred_element_type=jnp.float32), 0.0
        ).astype(jnp.bfloat16)
        partial_out = jnp.dot(hidden, w_down[0, 0], preferred_element_type=jnp.float32).astype(
            jnp.bfloat16
        )
        returned = lax.all_to_all(
            partial_out.reshape(received.shape), "expert", split_axis=0, concat_axis=0, tiled=True
        )
        combined = returned[0::2].astype(jnp.float32) + returned[1::2].astype(jnp.float32)
        expert_out = combined.astype(jnp.bfloat16).reshape(-1, model_width)
        result = (after_attn + combine(expert_out, target, usable, gate_pair)).astype(jnp.bfloat16)
        previous = lax.dynamic_index_in_dim(outputs, micro_index, 0, keepdims=False)
        outputs = lax.dynamic_update_index_in_dim(
            outputs, jnp.where(active, result, previous), micro_index, 0
        )
        if step_index + 1 < step_count:
            incoming = shifted(result, "segment", 1)
    return outputs.reshape(1, CAND_DEV * CAND_LEN, model_width)


def solution(mesh):
    return jax.shard_map(
        local,
        mesh=mesh,
        in_specs=(
            P("expert", None),
            P("expert"),
            P("segment", "expert", None),
            P(None, ("segment", "expert"), None),
            P("segment", None),
            P("segment", None),
            P("segment", None, None),
            P("segment", None, None),
            P("segment", None, None),
            P("segment", "expert", None, None),
            P("segment", "expert", None, None),
        ),
        out_specs=P("segment", "expert", None),
        check_vma=False,
    )
```

profile of v0, /device:TPU:0, one launch (start us, length us, event | category | flops | bytes accessed | tf_op | source)
XLA Modules:
  0.0 404.3 jit_solution(7827296348007882474)
XLA Ops:
  2.5 6.3 %all-to-all-start = ((bf16[4,2,1024]{2,1,0:T(2,128)(2,1)}), bf16[4,2,1024]{2,1,0:T(2,128)(2,1)S(1)}, u32[]{:S(2)}, u32[]{:S(2)}) async-start(bf16[4,2,1024]{2,1,0:T(2,128)(2,1)} %reshape.824), calls=%async_computation | async-start | bytes 32768 | tf_op jit(solution)/shard_map/all_to_all | solution.py:76
  15.9 3.2 fusion.137
  19.2 9.3 %all-gather = bf16[32,1,2048]{2,1,0:T(2,128)(2,1)S(1)} all-gather(bf16[4,1,2048]{2,1,0:T(2,128)(2,1)S(1)} %reshape.825), channel_id=2, replica_groups=mesh['segment'=4,'expert'=8] {'expert'}, dimensions={0}, use_global_device_ids=true | all-gather | bytes 147456 | tf_op jit(solution)/shard_map/all_gather | solution.py:77
  34.6 3.6 all-to-all-start.1
  43.9 12.4 %all-to-all-done.1 = bf16[8,40,2048]{2,1,0:T(8,128)(2,1)S(1)} async-done(((bf16[8,40,2048]{2,1,0:T(8,128)(2,1)}), bf16[8,40,2048]{2,1,0:T(8,128)(2,1)S(1)}, u32[]{:S(2)}, u32[]{:S(2)}) %all-to-all-start.1) | async-done | bytes 1310752 | tf_op jit(solution)/shard_map/all_to_all | solution.py:121
  56.3 12.4 %fusion.75 = bf16[320,2048]{1,0:T(8,128)(2,1)} fusion(bf16[1,1,2048,2048]{3,2,1,0:T(8,128)(2,1)} %param.23, bf16[320,2048]{1,0:T(8,128)(2,1)S(1)} %bitcast.391, bf16[1,1,2048,2048]{3,2,1,0:T(8,128)(2,1)} %param.22), kind=kOutput, calls=%fused_computation.60 | convolution fusion | flops 5370675200 | bytes 19398656 | tf_op jit(solution)/shard_map/dot_general | solution.py:126
  68.7 4.1 %all-to-all-start.2 = ((bf16[8,40,2048]{2,1,0:T(8,128)(2,1)}), bf16[8,40,2048]{2,1,0:T(8,128)(2,1)S(1)}, u32[]{:S(2)}, u32[]{:S(2)}) async-start(bf16[8,40,2048]{2,1,0:T(8,128)(2,1)} %bitcast.392), calls=%async_computation.2 | async-start | bytes 2621440 | tf_op jit(solution)/shard_map/all_to_all | solution.py:129
  75.6 15.3 %all-to-all-done.2 = bf16[8,40,2048]{2,1,0:T(8,128)(2,1)S(1)} async-done(((bf16[8,40,2048]{2,1,0:T(8,128)(2,1)}), bf16[8,40,2048]{2,1,0:T(8,128)(2,1)S(1)}, u32[]{:S(2)}, u32[]{:S(2)}) %all-to-all-start.2) | async-done | bytes 1310752 | tf_op jit(solution)/shard_map/all_to_all | solution.py:129
  95.3 3.9 collective-permute-start
  109.0 21.7 %all_to_all.62 = bf16[8,40,2048]{2,1,0:T(8,128)(2,1)S(1)} all-to-all(bf16[8,40,2048]{2,1,0:T(8,128)(2,1)S(1)} %bitcast.381), channel_id=1, replica_groups=mesh['segment'=4,'expert'=8] {'expert'}, dimensions={0} | all-to-all | bytes 2621440 | tf_op jit(solution)/shard_map/all_to_all | solution.py:121
  130.7 12.4 %fusion.78 = bf16[320,2048]{1,0:T(8,128)(2,1)} fusion(bf16[1,1,2048,2048]{3,2,1,0:T(8,128)(2,1)} %param.23, bf16[320,2048]{1,0:T(8,128)(2,1)S(1)} %bitcast.396, bf16[1,1,2048,2048]{3,2,1,0:T(8,128)(2,1)} %param.22), kind=kOutput, calls=%fused_computation.61 | convolution fusion | flops 5370675200 | bytes 19398656 | tf_op jit(solution)/shard_map/dot_general | solution.py:126
  143.1 3.7 all-to-all-start.4
  150.0 14.9 %all-to-all-done.4 = bf16[8,40,2048]{2,1,0:T(8,128)(2,1)S(1)} async-done(((bf16[8,40,2048]{2,1,0:T(8,128)(2,1)}), bf16[8,40,2048]{2,1,0:T(8,128)(2,1)S(1)}, u32[]{:S(2)}, u32[]{:S(2)}) %all-to-all-start.4) | async-done | bytes 1310752 | tf_op jit(solution)/shard_map/all_to_all | solution.py:129
  170.1 4.4 %collective-permute-start.1 = (bf16[64,2048]{1,0:T(8,128)(2,1)S(1)}, bf16[64,2048]{1,0:T(8,128)(2,1)S(1)}, u32[]{:S(2)}, u32[]{:S(2)}) collective-permute-start(bf16[64,2048]{1,0:T(8,128)(2,1)S(1)} %get-tuple-element.42), channel_id=1, source_target_pairs={{0,8},{8,16},{16,24},{1,9},{9,17},{17,25},{2,10},{10,18},{18,26},{... | collective-permute-start | bytes 786440 | tf_op jit(solution)/shard_map/ppermute | solution.py:19
  174.5 3.8 collective-permute-done.1
  187.5 3.7 all-to-all-start.5
  194.3 15.1 %all-to-all-done.5 = bf16[8,40,2048]{2,1,0:T(8,128)(2,1)S(1)} async-done(((bf16[8,40,2048]{2,1,0:T(8,128)(2,1)}), bf16[8,40,2048]{2,1,0:T(8,128)(2,1)S(1)}, u32[]{:S(2)}, u32[]{:S(2)}) %all-to-all-start.5) | async-done | bytes 1310752 | tf_op jit(solution)/shard_map/all_to_all | solution.py:121
  209.4 12.4 %fusion.81 = bf16[320,2048]{1,0:T(8,128)(2,1)} fusion(bf16[1,1,2048,2048]{3,2,1,0:T(8,128)(2,1)} %param.23, bf16[320,2048]{1,0:T(8,128)(2,1)S(1)} %bitcast.395, bf16[1,1,2048,2048]{3,2,1,0:T(8,128)(2,1)} %param.22), kind=kOutput, calls=%fused_computation.62 | convolution fusion | flops 5370675200 | bytes 19398656 | tf_op jit(solution)/shard_map/dot_general | solution.py:126
  221.8 3.9 all-to-all-start.6
  232.0 12.0 %all-to-all-done.6 = bf16[8,40,2048]{2,1,0:T(8,128)(2,1)S(1)} async-done(((bf16[8,40,2048]{2,1,0:T(8,128)(2,1)}), bf16[8,40,2048]{2,1,0:T(8,128)(2,1)S(1)}, u32[]{:S(2)}, u32[]{:S(2)}) %all-to-all-start.6) | async-done | bytes 1310752 | tf_op jit(solution)/shard_map/all_to_all | solution.py:129
  249.0 4.4 %collective-permute-start.2 = (bf16[64,2048]{1,0:T(8,128)(2,1)S(1)}, bf16[64,2048]{1,0:T(8,128)(2,1)S(1)}, u32[]{:S(2)}, u32[]{:S(2)}) collective-permute-start(bf16[64,2048]{1,0:T(8,128)(2,1)S(1)} %get-tuple-element.33), channel_id=1, source_target_pairs={{0,8},{8,16},{16,24},{1,9},{9,17},{17,25},{2,10},{10,18},{18,26},{... | collective-permute-start | bytes 786440 | tf_op jit(solution)/shard_map/ppermute | solution.py:19
  254.1 3.2 collective-permute-done.2
  265.4 21.7 %all_to_all.63 = bf16[8,40,2048]{2,1,0:T(8,128)(2,1)S(1)} all-to-all(bf16[8,40,2048]{2,1,0:T(8,128)(2,1)S(1)} %bitcast.382), channel_id=1, replica_groups=mesh['segment'=4,'expert'=8] {'expert'}, dimensions={0} | all-to-all | bytes 2621440 | tf_op jit(solution)/shard_map/all_to_all | solution.py:121
  287.0 12.4 %fusion.84 = bf16[320,2048]{1,0:T(8,128)(2,1)} fusion(bf16[1,1,2048,2048]{3,2,1,0:T(8,128)(2,1)} %param.23, bf16[320,2048]{1,0:T(8,128)(2,1)S(1)} %bitcast.397, bf16[1,1,2048,2048]{3,2,1,0:T(8,128)(2,1)} %param.22), kind=kOutput, calls=%fused_computation.63 | convolution fusion | flops 5370675200 | bytes 19398656 | tf_op jit(solution)/shard_map/dot_general | solution.py:126
  299.4 3.8 all-to-all-start.8
  306.5 15.0 %all-to-all-done.8 = bf16[8,40,2048]{2,1,0:T(8,128)(2,1)S(1)} async-done(((bf16[8,40,2048]{2,1,0:T(8,128)(2,1)}), bf16[8,40,2048]{2,1,0:T(8,128)(2,1)S(1)}, u32[]{:S(2)}, u32[]{:S(2)}) %all-to-all-start.8) | async-done | bytes 1310752 | tf_op jit(solution)/shard_map/all_to_all | solution.py:129
  326.5 4.4 %collective-permute-start.3 = (bf16[64,2048]{1,0:T(8,128)(2,1)S(1)}, bf16[64,2048]{1,0:T(8,128)(2,1)S(1)}, u32[]{:S(2)}, u32[]{:S(2)}) collective-permute-start(bf16[64,2048]{1,0:T(8,128)(2,1)S(1)} %get-tuple-element.24), channel_id=1, source_target_pairs={{0,8},{8,16},{16,24},{1,9},{9,17},{17,25},{2,10},{10,18},{18,26},{... | collective-permute-start | bytes 786440 | tf_op jit(solution)/shard_map/ppermute | solution.py:19
  330.9 3.8 collective-permute-done.3
  342.9 21.7 %all_to_all.64 = bf16[8,40,2048]{2,1,0:T(8,128)(2,1)S(1)} all-to-all(bf16[8,40,2048]{2,1,0:T(8,128)(2,1)S(1)} %bitcast.383), channel_id=1, replica_groups=mesh['segment'=4,'expert'=8] {'expert'}, dimensions={0} | all-to-all | bytes 2621440 | tf_op jit(solution)/shard_map/all_to_all | solution.py:121
  364.5 12.4 %fusion.87 = bf16[320,2048]{1,0:T(8,128)(2,1)} fusion(bf16[1,1,2048,2048]{3,2,1,0:T(8,128)(2,1)} %param.23, bf16[320,2048]{1,0:T(8,128)(2,1)S(1)} %bitcast.398, bf16[1,1,2048,2048]{3,2,1,0:T(8,128)(2,1)} %param.22), kind=kOutput, calls=%fused_computation.64 | convolution fusion | flops 5370675200 | bytes 19398656 | tf_op jit(solution)/shard_map/dot_general | solution.py:126
  376.9 4.0 all-to-all-start.10
  381.7 17.4 %all-to-all-done.10 = bf16[8,40,2048]{2,1,0:T(8,128)(2,1)S(1)} async-done(((bf16[8,40,2048]{2,1,0:T(8,128)(2,1)}), bf16[8,40,2048]{2,1,0:T(8,128)(2,1)S(1)}, u32[]{:S(2)}, u32[]{:S(2)}) %all-to-all-start.10) | async-done | bytes 1310752 | tf_op jit(solution)/shard_map/all_to_all | solution.py:129
  (327 shorter events, 99.3 us)
Async XLA Ops:
  0.0 74.7 %copy-start = (bf16[1,2048,4]{1,2,0:T(4,128)(2,1)S(1)}, bf16[1,2048,4]{1,2,0:T(4,128)(2,1)}, u32[]{:S(2)}) copy-start(bf16[1,2048,4]{1,2,0:T(4,128)(2,1)} %param.21) | copy-start | bytes 49156
  2.5 16.6 %all-to-all-start = ((bf16[4,2,1024]{2,1,0:T(2,128)(2,1)}), bf16[4,2,1024]{2,1,0:T(2,128)(2,1)S(1)}, u32[]{:S(2)}, u32[]{:S(2)}) async-start(bf16[4,2,1024]{2,1,0:T(2,128)(2,1)} %reshape.824), calls=%async_computation | async-start | bytes 32768 | tf_op jit(solution)/shard_map/all_to_all | solution.py:76
  15.9 13.6 %copy-start.2 = (bf16[128,2048]{1,0:T(8,128)(2,1)S(1)}, bf16[128,2048]{1,0:T(8,128)(2,1)}, u32[]{:S(2)}) copy-start(bf16[128,2048]{1,0:T(8,128)(2,1)} %param.13) | copy-start | bytes 1572868
  34.6 21.7 %all-to-all-start.1 = ((bf16[8,40,2048]{2,1,0:T(8,128)(2,1)}), bf16[8,40,2048]{2,1,0:T(8,128)(2,1)S(1)}, u32[]{:S(2)}, u32[]{:S(2)}) async-start(bf16[8,40,2048]{2,1,0:T(8,128)(2,1)} %bitcast.10), calls=%async_computation.1 | async-start | bytes 2621440 | tf_op jit(solution)/shard_map/all_to_all | solution.py:121
  43.6 25.1 %copy-start.36 = (pred[64]{0:T(512)(128)(4,1)}, pred[64]{0:T(512)(128)(4,1)S(1)}, u32[]{:S(2)}) copy-start(pred[64]{0:T(512)(128)(4,1)S(1)} %iota_compare_fusion.27) | copy-start | bytes 196
  68.7 22.2 %all-to-all-start.2 = ((bf16[8,40,2048]{2,1,0:T(8,128)(2,1)}), bf16[8,40,2048]{2,1,0:T(8,128)(2,1)S(1)}, u32[]{:S(2)}, u32[]{:S(2)}) async-start(bf16[8,40,2048]{2,1,0:T(8,128)(2,1)} %bitcast.392), calls=%async_computation.2 | async-start | bytes 2621440 | tf_op jit(solution)/shard_map/all_to_all | solution.py:129
  92.4 6.9 %copy-start.30 = (s32[1,64,2]{1,2,0:T(2,128)S(1)}, s32[1,64,2]{1,2,0:T(2,128)}, u32[]{:S(2)}) copy-start(s32[1,64,2]{1,2,0:T(2,128)} %copy.191) | copy-start | bytes 1540
  92.4 6.9 %copy-start.34 = (s32[1,64,2]{1,2,0:T(2,128)S(1)}, s32[1,64,2]{1,2,0:T(2,128)}, u32[]{:S(2)}) copy-start(s32[1,64,2]{1,2,0:T(2,128)} %copy.180) | copy-start | bytes 1540
  92.5 11.1 %copy-start.9 = (f32[1,2048]{1,0:T(1,128)S(1)}, f32[1,2048]{1,0:T(1,128)}, u32[]{:S(2)}) copy-start(f32[1,2048]{1,0:T(1,128)} %param.17) | copy-start | bytes 24580
  92.8 10.8 %copy-start.1 = (bf16[1,2048,1024]{2,1,0:T(8,128)(2,1)S(1)}, bf16[1,2048,1024]{2,1,0:T(8,128)(2,1)}, u32[]{:S(2)}) copy-start(bf16[1,2048,1024]{2,1,0:T(8,128)(2,1)} %param.19) | copy-start | bytes 12582916
  95.3 7.8 %collective-permute-start = (bf16[64,2048]{1,0:T(8,128)(2,1)S(1)}, bf16[64,2048]{1,0:T(8,128)(2,1)S(1)}, u32[]{:S(2)}, u32[]{:S(2)}) collective-permute-start(bf16[64,2048]{1,0:T(8,128)(2,1)S(1)} %get-tuple-element.51), channel_id=1, source_target_pairs={{0,8},{8,16},{16,24},{1,9},{9,17},{17,25},{2,10},{10,18},{18,26},{... | collective-permute-start | bytes 786440 | tf_op jit(solution)/shard_map/ppermute | solution.py:19
  143.1 21.9 %all-to-all-start.4 = ((bf16[8,40,2048]{2,1,0:T(8,128)(2,1)}), bf16[8,40,2048]{2,1,0:T(8,128)(2,1)S(1)}, u32[]{:S(2)}, u32[]{:S(2)}) async-start(bf16[8,40,2048]{2,1,0:T(8,128)(2,1)} %bitcast.393), calls=%async_computation.4 | async-start | bytes 2621440 | tf_op jit(solution)/shard_map/all_to_all | solution.py:129
  166.4 8.1 %copy-start.52 = (s32[64,2]{0,1:T(2,128)S(1)}, s32[64,2]{0,1:T(2,128)}, u32[]{:S(2)}) copy-start(s32[64,2]{0,1:T(2,128)} %get-tuple-element.38) | copy-start | bytes 1540
  166.4 12.4 %copy-start.10 = (f32[1,2048]{1,0:T(1,128)S(1)}, f32[1,2048]{1,0:T(1,128)}, u32[]{:S(2)}) copy-start(f32[1,2048]{1,0:T(1,128)} %param.17) | copy-start | bytes 24580
  170.1 8.3 %collective-permute-start.1 = (bf16[64,2048]{1,0:T(8,128)(2,1)S(1)}, bf16[64,2048]{1,0:T(8,128)(2,1)S(1)}, u32[]{:S(2)}, u32[]{:S(2)}) collective-permute-start(bf16[64,2048]{1,0:T(8,128)(2,1)S(1)} %get-tuple-element.42), channel_id=1, source_target_pairs={{0,8},{8,16},{16,24},{1,9},{9,17},{17,25},{2,10},{10,18},{18,26},{... | collective-permute-start | bytes 786440 | tf_op jit(solution)/shard_map/ppermute | solution.py:19
  186.3 7.3 %copy-start.7 = (s32[1,64,2]{2,1,0:T(8,128)S(1)}, s32[1,64,2]{2,1,0:T(8,128)}, u32[]{:S(2)}) copy-start(s32[1,64,2]{2,1,0:T(8,128)} %get-tuple-element.59) | copy-start | bytes 1540
  187.5 21.9 %all-to-all-start.5 = ((bf16[8,40,2048]{2,1,0:T(8,128)(2,1)}), bf16[8,40,2048]{2,1,0:T(8,128)(2,1)S(1)}, u32[]{:S(2)}, u32[]{:S(2)}) async-start(bf16[8,40,2048]{2,1,0:T(8,128)(2,1)} %bitcast.42), calls=%async_computation.5 | async-start | bytes 2621440 | tf_op jit(solution)/shard_map/all_to_all | solution.py:121
  221.8 8.5 %copy-start.31 = (s32[1,64,2]{1,2,0:T(2,128)S(1)}, s32[1,64,2]{1,2,0:T(2,128)}, u32[]{:S(2)}) copy-start(s32[1,64,2]{1,2,0:T(2,128)} %copy.191) | copy-start | bytes 1540
  221.8 22.1 %all-to-all-start.6 = ((bf16[8,40,2048]{2,1,0:T(8,128)(2,1)}), bf16[8,40,2048]{2,1,0:T(8,128)(2,1)S(1)}, u32[]{:S(2)}, u32[]{:S(2)}) async-start(bf16[8,40,2048]{2,1,0:T(8,128)(2,1)} %bitcast.389), calls=%async_computation.6 | async-start | bytes 2621440 | tf_op jit(solution)/shard_map/all_to_all | solution.py:129
  245.3 8.1 %copy-start.32 = (s32[1,64,2]{1,2,0:T(2,128)S(1)}, s32[1,64,2]{1,2,0:T(2,128)}, u32[]{:S(2)}) copy-start(s32[1,64,2]{1,2,0:T(2,128)} %copy.213) | copy-start | bytes 1540
  245.3 8.1 %copy-start.35 = (s32[1,64,2]{1,2,0:T(2,128)S(1)}, s32[1,64,2]{1,2,0:T(2,128)}, u32[]{:S(2)}) copy-start(s32[1,64,2]{1,2,0:T(2,128)} %copy.202) | copy-start | bytes 1540
  245.3 8.1 %copy-start.40 = (pred[64]{0:T(512)(128)(4,1)S(1)}, pred[64]{0:T(512)(128)(4,1)}, u32[]{:S(2)}) copy-start(pred[64]{0:T(512)(128)(4,1)} %copy-done.39) | copy-start | bytes 196
  245.3 8.1 %copy-start.43 = (pred[64]{0:T(512)(128)(4,1)S(1)}, pred[64]{0:T(512)(128)(4,1)}, u32[]{:S(2)}) copy-start(pred[64]{0:T(512)(128)(4,1)} %copy-done.42) | copy-start | bytes 196
  245.4 8.1 %copy-start.49 = (s32[64,2]{0,1:T(2,128)S(1)}, s32[64,2]{0,1:T(2,128)}, u32[]{:S(2)}) copy-start(s32[64,2]{0,1:T(2,128)} %copy.204) | copy-start | bytes 1540
  245.4 8.1 %copy-start.50 = (s32[64,2]{0,1:T(2,128)S(1)}, s32[64,2]{0,1:T(2,128)}, u32[]{:S(2)}) copy-start(s32[64,2]{0,1:T(2,128)} %copy.215) | copy-start | bytes 1540
  245.4 12.4 %copy-start.11 = (f32[1,2048]{1,0:T(1,128)S(1)}, f32[1,2048]{1,0:T(1,128)}, u32[]{:S(2)}) copy-start(f32[1,2048]{1,0:T(1,128)} %param.17) | copy-start | bytes 24580
  249.0 8.3 %collective-permute-start.2 = (bf16[64,2048]{1,0:T(8,128)(2,1)S(1)}, bf16[64,2048]{1,0:T(8,128)(2,1)S(1)}, u32[]{:S(2)}, u32[]{:S(2)}) collective-permute-start(bf16[64,2048]{1,0:T(8,128)(2,1)S(1)} %get-tuple-element.33), channel_id=1, source_target_pairs={{0,8},{8,16},{16,24},{1,9},{9,17},{17,25},{2,10},{10,18},{18,26},{... | collective-permute-start | bytes 786440 | tf_op jit(solution)/shard_map/ppermute | solution.py:19
  299.4 22.0 %all-to-all-start.8 = ((bf16[8,40,2048]{2,1,0:T(8,128)(2,1)}), bf16[8,40,2048]{2,1,0:T(8,128)(2,1)S(1)}, u32[]{:S(2)}, u32[]{:S(2)}) async-start(bf16[8,40,2048]{2,1,0:T(8,128)(2,1)} %bitcast.394), calls=%async_computation.8 | async-start | bytes 2621440 | tf_op jit(solution)/shard_map/all_to_all | solution.py:129
  322.8 8.1 %copy-start.53 = (s32[64,2]{0,1:T(2,128)S(1)}, s32[64,2]{0,1:T(2,128)}, u32[]{:S(2)}) copy-start(s32[64,2]{0,1:T(2,128)} %get-tuple-element.20) | copy-start | bytes 1540
  322.8 12.4 %copy-start.12 = (f32[1,2048]{1,0:T(1,128)S(1)}, f32[1,2048]{1,0:T(1,128)}, u32[]{:S(2)}) copy-start(f32[1,2048]{1,0:T(1,128)} %param.17) | copy-start | bytes 24580
  326.5 8.3 %collective-permute-start.3 = (bf16[64,2048]{1,0:T(8,128)(2,1)S(1)}, bf16[64,2048]{1,0:T(8,128)(2,1)S(1)}, u32[]{:S(2)}, u32[]{:S(2)}) collective-permute-start(bf16[64,2048]{1,0:T(8,128)(2,1)S(1)} %get-tuple-element.24), channel_id=1, source_target_pairs={{0,8},{8,16},{16,24},{1,9},{9,17},{17,25},{2,10},{10,18},{18,26},{... | collective-permute-start | bytes 786440 | tf_op jit(solution)/shard_map/ppermute | solution.py:19
  376.9 22.1 %all-to-all-start.10 = ((bf16[8,40,2048]{2,1,0:T(8,128)(2,1)}), bf16[8,40,2048]{2,1,0:T(8,128)(2,1)S(1)}, u32[]{:S(2)}, u32[]{:S(2)}) async-start(bf16[8,40,2048]{2,1,0:T(8,128)(2,1)} %bitcast.390), calls=%async_computation.10 | async-start | bytes 2621440 | tf_op jit(solution)/shard_map/all_to_all | solution.py:129
  (36 other events, 129.8 us)
where the time goes:
time: 412 us; the launch traced here: 404 us
  waiting for transfers between devices  116 us (28%)
  matrix products  95.9 us (23%)
  blocking collectives  74.3 us (18%)
  starting transfers between devices  50.3 us (12%)
  local copies, waits for them, and re-layouts  33.5 us (8%)
  other arithmetic  32 us (8%)
    all_to_all x5, waiting for transfers between devices, local(): lax.all_to_all(partial_out.reshape(received.shape), 'expert', split_axis=...  74.6 us
    all_to_all x3, blocking collectives, local(): lax.all_to_all(outgoing, 'expert', split_axis=0, concat_axis=0, tiled=True)  65 us
    dot_general x5, matrix products, local(): jnp.dot(hidden, w_down[0, 0], preferred_element_type=jnp.float32)  62 us
    all_to_all x2, waiting for transfers between devices, local(): lax.all_to_all(outgoing, 'expert', split_axis=0, concat_axis=0, tiled=True)  27.6 us
    all_to_all x5, starting transfers between devices, local(): lax.all_to_all(partial_out.reshape(received.shape), 'expert', split_axis=...  19.6 us
    ppermute x4, starting transfers between devices, shifted(): return lax.ppermute(shard, axis, pairs)  17.1 us
    dot_general x5, matrix products, local(): jnp.dot(context, w_out[0], preferred_element_type=jnp.float32)  15.8 us
    reduce_sum x5, other arithmetic, combine(): return jnp.sum(picked * weight[:, :, None], axis=1)  14.2 us
  transfers between devices with their start and end apart: 12, of which 11 were waited for; matrix products, arithmetic and copies ran while one was open for 9% of the time, Pallas kernels for 0%

commit v1 on v0

v1 whole, which is shorter than its diff:
```python
import functools
import math

import jax
import jax.numpy as jnp
from jax import lax
from jax.experimental import pallas as pl
from jax.experimental.pallas import tpu as pltpu
from jax.sharding import PartitionSpec as P

HEAD_DIM = 128
CAND_LEN = 64
CAND_DEV = 2
HIDDEN_CHUNK = 512
MIB = 1 << 20

EPSILON = 1e-05

VMEM = pl.BlockSpec(memory_space=pltpu.VMEM)
SMEM = pl.BlockSpec(memory_space=pltpu.SMEM)
ANY = pl.BlockSpec(memory_space=pl.ANY)
F32 = jnp.float32
BF16 = jnp.bfloat16


def normalize(carried, gain_row):
    average = jnp.mean(carried, axis=-1, keepdims=True)
    centered = carried - average
    variance = jnp.mean(centered * centered, axis=-1, keepdims=True)
    return gain_row * centered * lax.rsqrt(variance + EPSILON)


def dot(left, right, contract=((1,), (0,))):
    return lax.dot_general(left, right, (contract, ((), ())), preferred_element_type=F32)


def attend_kernel(
    step, capacity, segment, cand_len, *refs
):
    if step == 0:
        fresh, refs = refs[0], refs[1:]
    elif step == 1:
        fresh, incoming, refs = refs[0], refs[1], refs[2:]
    else:
        incoming, refs = refs[0], refs[1:]
    (routes, cached, attn_gain, ffn_gain, w_query, w_out, router_t,
     after_ref, outgoing, weights, query_buf, out_buf, context, sems) = refs
    query_copy = pltpu.make_async_copy(w_query, query_buf, sems.at[0])
    out_copy = pltpu.make_async_copy(w_out, out_buf, sems.at[1])
    query_copy.start()
    out_copy.start()

    if step == 0:
        current = fresh[...]
    elif step == 1:
        current = jnp.where(segment[0] == 0, fresh[...], incoming[...])
    else:
        current = incoming[...]
    carried = current.astype(F32)
    normed = normalize(carried, attn_gain[...]).astype(BF16)
    query_copy.wait()
    queries = dot(normed, query_buf[...]).astype(BF16)
    head_total = queries.shape[1]
    scale = 1.0 / math.sqrt(HEAD_DIM)
    for start in range(0, head_total, HEAD_DIM):
        lanes = slice(start, start + HEAD_DIM)
        scores = dot(queries[:, lanes], cached[:, lanes], ((1,), (1,))) * scale
        exponent = jnp.exp(scores - jnp.max(scores, axis=1, keepdims=True))
        share = (exponent / jnp.sum(exponent, axis=1, keepdims=True)).astype(BF16)
        values = cached[:, head_total + start : head_total + start + HEAD_DIM]
        context[:, lanes] = dot(share, values).astype(BF16)
    out_copy.wait()
    after_attn = carried + dot(context[...], out_buf[...])
    after_ref[...] = after_attn
    ffn_input = normalize(after_attn, ffn_gain[...]).astype(BF16)

    rows, experts = after_attn.shape[0], router_t.shape[0]
    logits = dot(ffn_input, router_t[...], ((1,), (1,)))
    micro = jnp.clip(step - segment[0], 0, CAND_DEV - 1)
    live = lax.broadcasted_iota(jnp.int32, (rows, 1), 0) < cand_len[micro]
    route = routes[micro]
    labels = lax.broadcasted_iota(jnp.int32, (rows, experts), 1)
    first, second = route[:, 0:1] == labels, route[:, 1:2] == labels
    logit_first = jnp.sum(jnp.where(first, logits, 0.0), axis=1, keepdims=True)
    logit_second = jnp.sum(jnp.where(second, logits, 0.0), axis=1, keepdims=True)
    gate_first = jax.nn.sigmoid(logit_first - logit_second)
    gate_second = 1.0 - gate_first
    named = jnp.where((first | second) & live, 1.0, 0.0).astype(BF16)
    earlier = lax.broadcasted_iota(jnp.int32, (rows, rows), 1) < lax.broadcasted_iota(
        jnp.int32, (rows, rows), 0
    )
    before = dot(jnp.where(earlier, 1.0, 0.0).astype(BF16), named)
    slots = lax.broadcasted_iota(jnp.int32, (rows, experts * capacity), 1)
    chosen = []
    for mask, column in ((first, 0), (second, 1)):
        slot = jnp.sum(jnp.where(mask, before, 0.0), axis=1, keepdims=True).astype(jnp.int32)
        target = route[:, column : column + 1] * capacity + slot
        chosen.append((slots == target) & live)
    select = jnp.where(chosen[0] | chosen[1], 1.0, 0.0).astype(BF16)
    outgoing[...] = dot(select, ffn_input, ((0,), (0,))).astype(BF16)
    weights[...] = jnp.where(chosen[0], gate_first, 0.0) + jnp.where(chosen[1], gate_second, 0.0)


def attend(step, capacity, segment, cand_len, sources, routes, cached, gains, mats):
    w_query, w_out, router_t = mats
    width, head_total = w_query.shape
    slot_count = router_t.shape[0] * capacity
    specs = [SMEM, SMEM]
    for source in sources:
        if source.shape[0] == CAND_LEN:
            specs.append(VMEM)
        else:
            specs.append(pl.BlockSpec((CAND_LEN, width), lambda i: (min(step, CAND_DEV - 1), 0)))
    return pl.pallas_call(
        functools.partial(attend_kernel, step, capacity),
        grid=(1,),
        in_specs=specs + [VMEM, VMEM, VMEM, VMEM, ANY, ANY, VMEM],
        out_specs=[VMEM, VMEM, VMEM],
        out_shape=[
            jax.ShapeDtypeStruct((CAND_LEN, width), F32),
            jax.ShapeDtypeStruct((slot_count, width), BF16),
            jax.ShapeDtypeStruct((CAND_LEN, slot_count), F32),
        ],
        scratch_shapes=[
            pltpu.VMEM(w_query.shape, BF16),
            pltpu.VMEM(w_out.shape, BF16),
            pltpu.VMEM((CAND_LEN, head_total), BF16),
            pltpu.SemaphoreType.DMA((2,)),
        ],
        compiler_params=pltpu.CompilerParams(vmem_limit_bytes=24 * MIB),
        cost_estimate=pl.CostEstimate(
            flops=6 * CAND_LEN * width * head_total,
            bytes_accessed=4 * width * head_total + 8 * CAND_LEN * width,
            transcendentals=0,
        ),
        name="attend",
    )(segment, cand_len, *sources, routes, cached, *gains, w_query, w_out, router_t)


def expert_kernel(rows, own_in, own_down, other_in, other_down, served, in_buf, down_buf, total, in_sems, down_sems):
    chunks = in_buf.shape[0] // 2
    size = in_buf.shape[2]

    def copies(first_mat, second_mat, base, chunk):
        units = pl.ds(pl.multiple_of(chunk * size, size), size)
        slot = base + chunk
        return (
            pltpu.make_async_copy(first_mat.at[:, units], in_buf.at[slot], in_sems.at[slot]),
            pltpu.make_async_copy(second_mat.at[units, :], down_buf.at[slot], down_sems.at[slot]),
        )

    halves = ((own_in, own_down, 0), (other_in, other_down, chunks))
    for first_mat, second_mat, base in halves:
        for chunk in range(chunks):
            for copy in copies(first_mat, second_mat, base, chunk):
                copy.start()
    total[...] = jnp.zeros_like(total)
    for first_mat, second_mat, base in halves:

        @pl.loop(0, chunks)
        def _(chunk):
            first_copy, second_copy = copies(first_mat, second_mat, base, chunk)
            first_copy.wait()
            hidden = jnp.maximum(dot(rows[...], in_buf[base + chunk]), 0.0).astype(BF16)
            second_copy.wait()
            total[...] += dot(hidden, down_buf[base + chunk])

    served[...] = total[...].astype(BF16)


def expert_rows(rows, own_in, own_down, other_in, other_down):
    count, width = rows.shape
    units = own_in.shape[1]
    chunks = 2 * units // HIDDEN_CHUNK
    return pl.pallas_call(
        expert_kernel,
        in_specs=[VMEM, ANY, ANY, ANY, ANY],
        out_specs=VMEM,
        out_shape=jax.ShapeDtypeStruct(rows.shape, BF16),
        scratch_shapes=[
            pltpu.VMEM((chunks, width, HIDDEN_CHUNK), BF16),
            pltpu.VMEM((chunks, HIDDEN_CHUNK, width), BF16),
            pltpu.VMEM((count, width), F32),
            pltpu.SemaphoreType.DMA((chunks,)),
            pltpu.SemaphoreType.DMA((chunks,)),
        ],
        compiler_params=pltpu.CompilerParams(vmem_limit_bytes=44 * MIB),
        cost_estimate=pl.CostEstimate(
            flops=8 * count * width * units,
            bytes_accessed=8 * width * units + 4 * count * width,
            transcendentals=0,
        ),
        name="experts",
    )(rows, own_in, own_down, other_in, other_down)


def combine_kernel(after_attn, weights, expert_out, result):
    gates = weights[...]
    coarse = gates.astype(BF16)
    fine = (gates - coarse.astype(F32)).astype(BF16)
    rows = expert_out[...]
    result[...] = (after_attn[...] + (dot(coarse, rows) + dot(fine, rows))).astype(BF16)


def combine(after_attn, weights, expert_out):
    return pl.pallas_call(
        combine_kernel,
        in_specs=[VMEM, VMEM, VMEM],
        out_specs=VMEM,
        out_shape=jax.ShapeDtypeStruct(after_attn.shape, BF16),
        compiler_params=pltpu.CompilerParams(vmem_limit_bytes=16 * MIB),
        cost_estimate=pl.CostEstimate(
            flops=4 * weights.size * after_attn.shape[1],
            bytes_accessed=6 * after_attn.size + 2 * expert_out.size,
            transcendentals=0,
        ),
        name="combine",
    )(after_attn, weights, expert_out)


def local(
    states, cand_len, routes, enc_kv, attn_gain, ffn_gain, w_query, w_out, w_router, w_in, w_down
):
    segment_index = lax.axis_index("segment")
    n_segment = lax.axis_size("segment")
    n_expert = lax.axis_size("expert")
    model_width = states.shape[1]
    experts = w_router.shape[2]
    capacity = 2 * ((5 * CAND_LEN + 4 * experts - 1) // (4 * experts))
    core_pairs = [(i, i ^ 1) for i in range(n_expert)]
    same_core = [list(range(core, n_expert, 2)) for core in range(2)]

    def exchange(rows):
        blocks = rows.reshape(experts, capacity, model_width)
        moved = lax.all_to_all(
            blocks, "expert", split_axis=0, concat_axis=0, axis_index_groups=same_core, tiled=True
        )
        return moved.reshape(rows.shape)

    spread = jnp.repeat(enc_kv[:, 0, :], n_expert, axis=0)
    cached = lax.all_to_all(
        spread, ("segment", "expert"), split_axis=0, concat_axis=0, tiled=True
    )
    own = (w_in[0, 0], w_down[0, 0])
    other = tuple(lax.ppermute(mat, "expert", core_pairs) for mat in own)

    segment = segment_index.astype(jnp.int32).reshape(1)
    route_all = routes[0].reshape(CAND_DEV, CAND_LEN, 2)
    mats = (w_query[0], w_out[0], w_router[0].T)
    outputs = jnp.zeros((CAND_DEV, CAND_LEN, model_width), BF16)
    step_count = CAND_DEV + n_segment - 1
    incoming = None
    for step in range(step_count):
        if step == 0:
            sources = (states,)
        elif step < CAND_DEV:
            sources = (states, incoming)
        else:
            sources = (incoming,)
        after_attn, outgoing, weights = attend(
            step, capacity, segment, cand_len, sources, route_all, cached,
            (attn_gain, ffn_gain), mats,
        )
        served = expert_rows(exchange(outgoing), *own, *other)
        result = combine(after_attn, weights, exchange(served))
        if step + 1 < step_count:
            incoming = lax.ppermute(
                result, "segment", [(i, i + 1) for i in range(n_segment - 1)]
            )
        micro_step = step - segment_index
        active = (micro_step >= 0) & (micro_step < CAND_DEV)
        micro_index = jnp.clip(micro_step, 0, CAND_DEV - 1)
        previous = lax.dynamic_index_in_dim(outputs, micro_index, 0, keepdims=False)
        outputs = lax.dynamic_update_index_in_dim(
            outputs, jnp.where(active, result, previous), micro_index, 0
        )
    return outputs.reshape(1, CAND_DEV * CAND_LEN, model_width)


def solution(mesh):
    return jax.shard_map(
        local,
        mesh=mesh,
        in_specs=(
            P("expert", None),
            P("expert"),
            P("segment", "expert", None),
            P(None, ("segment", "expert"), None),
            P("segment", None),
            P("segment", None),
            P("segment", None, None),
            P("segment", None, None),
            P("segment", None, None),
            P("segment", "expert", None, None),
            P("segment", "expert", None, None),
        ),
        out_specs=P("segment", "expert", None),
        check_vma=False,
    )
```

time: 412 us -> 265 us (0.64); the launches traced: 404 us -> 263 us
  matrix products: 95.9 us -> 0 us
  Pallas kernels: 0 us -> 75.3 us
  waiting for transfers between devices: 116 us -> 51.1 us
  other arithmetic: 32 us -> 0.99 us
  starting transfers between devices: 50.3 us -> 36.7 us
  blocking collectives: 74.3 us -> 65.8 us
    dot_general x30 -> x0, matrix products: 94.8 us -> none  [the longest x5 62 us: local(): jnp.dot(hidden, w_down[0, 0], preferred_element_type=jnp.float32)]
    pallas_call x0 -> x15, Pallas kernels: none -> 75.3 us  [the longest x5 51.2 us: expert_rows(): pl.pallas_call(expert_kernel, in_specs=[VMEM, ANY, ANY, ANY, ANY], out_sp...]
    all_to_all x8 -> x5, waiting for transfers between devices: 102 us -> 36.2 us  [the longest x4 28.8 us: exchange(): lax.all_to_all(blocks, 'expert', split_axis=0, concat_axis=0, axis_index_...]
    unnamed x119 -> x50, local copies, waits for them, and re-layouts: 3.35 us -> 32.4 us
    reduce_sum x25 -> x0, other arithmetic: 20.2 us -> none  [the longest x5 14.2 us: combine(): return jnp.sum(picked * weight[:, :, None], axis=1)]
    all_to_all x8 -> x5, starting transfers between devices: 33.1 us -> 21.3 us  [the longest x4 14 us: exchange(): lax.all_to_all(blocks, 'expert', split_axis=0, concat_axis=0, axis_index_...]
    all_gather x1 -> x0, blocking collectives: 9.32 us -> none  [local(): cached = lax.all_gather(layer_kv, 'expert', axis=1, tiled=True)]
    gather x10 -> x0, local copies, waits for them, and re-layouts: 7.39 us -> none  [combine(): jnp.take(expert_out, jnp.where(usable, target, 0), axis=0)]
  transfers between devices with their start and end apart: 12 -> 11, of which waited for: 11 -> 9; matrix products, arithmetic and copies ran while one was open for 9% -> 1% of each run, Pallas kernels for 0% -> 2%
where the time goes in v1:
time: 265 us; the launch traced here: 263 us
  Pallas kernels  75.3 us (28%)
  blocking collectives  65.8 us (25%)
  waiting for transfers between devices  51.1 us (19%)
  starting transfers between devices  36.7 us (14%)
  local copies, waits for them, and re-layouts  33.1 us (12%)
    all_to_all x6, blocking collectives, exchange(): lax.all_to_all(blocks, 'expert', split_axis=0, concat_axis=0, axis_index_...  65.8 us
    pallas_call x5, Pallas kernels, expert_rows(): pl.pallas_call(expert_kernel, in_specs=[VMEM, ANY, ANY, ANY, ANY], out_sp...  51.2 us
    unnamed x50, local copies, waits for them, and re-layouts  32.4 us
    all_to_all x4, waiting for transfers between devices, exchange(): lax.all_to_all(blocks, 'expert', split_axis=0, concat_axis=0, axis_index_...  28.8 us
    pallas_call x5, Pallas kernels, attend(): pl.pallas_call(functools.partial(attend_kernel, step, capacity), grid=(1,...  22.4 us
    ppermute x4, waiting for transfers between devices, local(): lax.ppermute(result, 'segment', [(i, i + 1) for i in range(n_segment - 1)])  14.9 us
    ppermute x4, starting transfers between devices, local(): lax.ppermute(result, 'segment', [(i, i + 1) for i in range(n_segment - 1)])  14.9 us
    all_to_all x4, starting transfers between devices, exchange(): lax.all_to_all(blocks, 'expert', split_axis=0, concat_axis=0, axis_index_...  14 us
  transfers between devices with their start and end apart: 11, of which 9 were waited for; matrix products, arithmetic and copies ran while one was open for 1% of the time, Pallas kernels for 2%

profile of v1, /device:TPU:0, one launch (start us, length us, event | category | flops | bytes accessed | tf_op | source)
XLA Modules:
  0.0 263.3 jit_solution(14592916142113916693)
XLA Ops:
  2.7 7.3 %all-to-all-start = ((bf16[32,2,1024]{2,1,0:T(2,128)(2,1)}), bf16[32,2,1024]{2,1,0:T(2,128)(2,1)S(1)}, u32[]{:S(2)}, u32[]{:S(2)}) async-start(bf16[32,2,1024]{2,1,0:T(2,128)(2,1)} %reshape.92), calls=%async_computation | async-start | bytes 262144 | tf_op jit(solution)/shard_map/all_to_all | solution.py:241
  10.8 7.4 %all-to-all-done = bf16[32,2,1024]{2,1,0:T(2,128)(2,1)S(1)} async-done(((bf16[32,2,1024]{2,1,0:T(2,128)(2,1)}), bf16[32,2,1024]{2,1,0:T(2,128)(2,1)S(1)}, u32[]{:S(2)}, u32[]{:S(2)}) %all-to-all-start) | async-done | bytes 131104 | tf_op jit(solution)/shard_map/all_to_all | solution.py:241
  27.0 4.1 %attend.5 = (f32[64,2048]{1,0:T(8,128)S(1)}, bf16[160,2048]{1,0:T(8,128)(2,1)S(1)}, f32[64,160]{1,0:T(8,128)S(1)}) custom-call(s32[1]{0:T(128)} %bitcast.segment, s32[2]{0:T(128)S(1)} %copy-done.20, bf16[128,2048]{1,0:T(8,128)(2,1)S(1)} %copy-done.13, s32[2,64,2]{2,1,0:T(8,128)S(1)} %bitcast.97, bf16[32,2048]{1,0:T(8,128)(2,1)S(1)} %bitcast.79, ...), custom_call_target="tpu_custom_call" | custom-call | flops 805306368 | bytes 9437184 | tf_op jit(solution)/shard_map/attend/pallas_call | solution.py:114
  31.2 13.0 %all_to_all.61 = bf16[4,40,2048]{2,1,0:T(8,128)(2,1)S(1)} all-to-all(bf16[4,40,2048]{2,1,0:T(8,128)(2,1)S(1)} %bitcast.104), channel_id=1, replica_groups={{0,2,4,6},{1,3,5,7},{8,10,12,14},{9,11,13,15},{16,18,20,22},{17,19,21,2..., dimensions={0} | all-to-all | bytes 1310720 | tf_op jit(solution)/shard_map/all_to_all | solution.py:235
  44.2 10.0 %experts.5 = bf16[160,2048]{1,0:T(8,128)(2,1)S(1)} custom-call(bf16[160,2048]{1,0:T(8,128)(2,1)S(1)} %bitcast.91, bf16[2048,2048]{1,0:T(8,128)(2,1)S(1)} %bitcast.64, bf16[2048,2048]{1,0:T(8,128)(2,1)} %bitcast.111, bf16[2048,2048]{1,0:T(8,128)(2,1)} %collective-permute-done.other_in, bf16[2048,2048]{1,0:T(8,128)(2,1)} %collective-permute-done.1.other_down), custom_call_target="tpu_custom_call" | custom-call | flops 5368709120 | bytes 34865152 | tf_op jit(solution)/shard_map/experts/pallas_call | solution.py:175
  54.2 11.8 %all_to_all.62 = bf16[4,40,2048]{2,1,0:T(8,128)(2,1)S(1)} all-to-all(bf16[4,40,2048]{2,1,0:T(8,128)(2,1)S(1)} %bitcast.92), channel_id=1, replica_groups={{0,2,4,6},{1,3,5,7},{8,10,12,14},{9,11,13,15},{16,18,20,22},{17,19,21,2..., dimensions={0} | all-to-all | bytes 1310720 | tf_op jit(solution)/shard_map/all_to_all | solution.py:235
  67.7 3.9 %collective-permute-done.2.refs_1_ = bf16[64,2048]{1,0:T(8,128)(2,1)S(1)} collective-permute-done((bf16[64,2048]{1,0:T(8,128)(2,1)S(1)}, bf16[64,2048]{1,0:T(8,128)(2,1)S(1)}, u32[]{:S(2)}, u32[]{:S(2)}) %collective-permute-start.2) | collective-permute-done | bytes 262176 | tf_op jit(solution)/shard_map/ppermute | solution.py:267
  73.8 4.2 %attend.6 = (f32[64,2048]{1,0:T(8,128)S(1)}, bf16[160,2048]{1,0:T(8,128)(2,1)S(1)}, f32[64,160]{1,0:T(8,128)S(1)}) custom-call(s32[1]{0:T(128)} %bitcast.segment, s32[2]{0:T(128)S(1)} %copy-done.20, bf16[128,2048]{1,0:T(8,128)(2,1)S(1)} %copy-done.13, bf16[64,2048]{1,0:T(8,128)(2,1)S(1)} %collective-permute-done.2.refs_1_, s32[2,64,2]{2,1,0:T(8,128)S(1)} %bitcast.98, ...), custom_call_target="tpu_custom_call" | custom-call | flops 805306368 | bytes 9437184 | tf_op jit(solution)/shard_map/attend/pallas_call | solution.py:114
  77.9 10.2 %all_to_all.63 = bf16[4,40,2048]{2,1,0:T(8,128)(2,1)S(1)} all-to-all(bf16[4,40,2048]{2,1,0:T(8,128)(2,1)S(1)} %bitcast.102), channel_id=1, replica_groups={{0,2,4,6},{1,3,5,7},{8,10,12,14},{9,11,13,15},{16,18,20,22},{17,19,21,2..., dimensions={0} | all-to-all | bytes 1310720 | tf_op jit(solution)/shard_map/all_to_all | solution.py:235
  91.5 9.9 %experts.6 = bf16[160,2048]{1,0:T(8,128)(2,1)S(1)} custom-call(bf16[160,2048]{1,0:T(8,128)(2,1)S(1)} %bitcast.93, bf16[2048,2048]{1,0:T(8,128)(2,1)S(1)} %bitcast.65, bf16[2048,2048]{1,0:T(8,128)(2,1)} %bitcast.112, bf16[2048,2048]{1,0:T(8,128)(2,1)} %collective-permute-done.other_in, bf16[2048,2048]{1,0:T(8,128)(2,1)} %collective-permute-done.1.other_down), custom_call_target="tpu_custom_call" | custom-call | flops 5368709120 | bytes 34865152 | tf_op jit(solution)/shard_map/experts/pallas_call | solution.py:175
  101.4 10.2 %all_to_all.64 = bf16[4,40,2048]{2,1,0:T(8,128)(2,1)S(1)} all-to-all(bf16[4,40,2048]{2,1,0:T(8,128)(2,1)S(1)} %bitcast.94), channel_id=1, replica_groups={{0,2,4,6},{1,3,5,7},{8,10,12,14},{9,11,13,15},{16,18,20,22},{17,19,21,2..., dimensions={0} | all-to-all | bytes 1310720 | tf_op jit(solution)/shard_map/all_to_all | solution.py:235
  112.0 4.6 %collective-permute-start.3 = (bf16[64,2048]{1,0:T(8,128)(2,1)S(1)}, bf16[64,2048]{1,0:T(8,128)(2,1)S(1)}, u32[]{:S(2)}, u32[]{:S(2)}) collective-permute-start(bf16[64,2048]{1,0:T(8,128)(2,1)S(1)} %combine.6), channel_id=1, source_target_pairs={{0,8},{8,16},{16,24},{1,9},{9,17},{17,25},{2,10},{10,18},{18,26},{... | collective-permute-start | bytes 786440 | tf_op jit(solution)/shard_map/ppermute | solution.py:267
  116.6 3.7 %collective-permute-done.3.refs_0_ = bf16[64,2048]{1,0:T(8,128)(2,1)S(1)} collective-permute-done((bf16[64,2048]{1,0:T(8,128)(2,1)S(1)}, bf16[64,2048]{1,0:T(8,128)(2,1)S(1)}, u32[]{:S(2)}, u32[]{:S(2)}) %collective-permute-start.3) | collective-permute-done | bytes 262176 | tf_op jit(solution)/shard_map/ppermute | solution.py:267
  122.4 4.1 %attend.7 = (f32[64,2048]{1,0:T(8,128)S(1)}, bf16[160,2048]{1,0:T(8,128)(2,1)S(1)}, f32[64,160]{1,0:T(8,128)S(1)}) custom-call(s32[1]{0:T(128)} %bitcast.segment, s32[2]{0:T(128)S(1)} %copy-done.20, bf16[64,2048]{1,0:T(8,128)(2,1)S(1)} %collective-permute-done.3.refs_0_, s32[2,64,2]{2,1,0:T(8,128)S(1)} %bitcast.99, bf16[32,2048]{1,0:T(8,128)(2,1)S(1)} %bitcast.81, ...), custom_call_target="tpu_custom_call" | custom-call | flops 805306368 | bytes 9437184 | tf_op jit(solution)/shard_map/attend/pallas_call | solution.py:114
  126.6 10.2 %all_to_all.65 = bf16[4,40,2048]{2,1,0:T(8,128)(2,1)S(1)} all-to-all(bf16[4,40,2048]{2,1,0:T(8,128)(2,1)S(1)} %bitcast.103), channel_id=1, replica_groups={{0,2,4,6},{1,3,5,7},{8,10,12,14},{9,11,13,15},{16,18,20,22},{17,19,21,2..., dimensions={0} | all-to-all | bytes 1310720 | tf_op jit(solution)/shard_map/all_to_all | solution.py:235
  136.8 9.8 %experts.7 = bf16[160,2048]{1,0:T(8,128)(2,1)S(1)} custom-call(bf16[160,2048]{1,0:T(8,128)(2,1)S(1)} %bitcast.95, bf16[2048,2048]{1,0:T(8,128)(2,1)S(1)} %bitcast.66, bf16[2048,2048]{1,0:T(8,128)(2,1)} %bitcast.113, bf16[2048,2048]{1,0:T(8,128)(2,1)} %collective-permute-done.other_in, bf16[2048,2048]{1,0:T(8,128)(2,1)} %collective-permute-done.1.other_down), custom_call_target="tpu_custom_call" | custom-call | flops 5368709120 | bytes 34865152 | tf_op jit(solution)/shard_map/experts/pallas_call | solution.py:175
  146.7 10.2 %all_to_all.66 = bf16[4,40,2048]{2,1,0:T(8,128)(2,1)S(1)} all-to-all(bf16[4,40,2048]{2,1,0:T(8,128)(2,1)S(1)} %bitcast.96), channel_id=1, replica_groups={{0,2,4,6},{1,3,5,7},{8,10,12,14},{9,11,13,15},{16,18,20,22},{17,19,21,2..., dimensions={0} | all-to-all | bytes 1310720 | tf_op jit(solution)/shard_map/all_to_all | solution.py:235
  157.3 4.4 %collective-permute-start.4 = (bf16[64,2048]{1,0:T(8,128)(2,1)S(1)}, bf16[64,2048]{1,0:T(8,128)(2,1)S(1)}, u32[]{:S(2)}, u32[]{:S(2)}) collective-permute-start(bf16[64,2048]{1,0:T(8,128)(2,1)S(1)} %combine.7), channel_id=1, source_target_pairs={{0,8},{8,16},{16,24},{1,9},{9,17},{17,25},{2,10},{10,18},{18,26},{... | collective-permute-start | bytes 786440 | tf_op jit(solution)/shard_map/ppermute | solution.py:267
  161.7 3.9 %collective-permute-done.4.refs_0_ = bf16[64,2048]{1,0:T(8,128)(2,1)S(1)} collective-permute-done((bf16[64,2048]{1,0:T(8,128)(2,1)S(1)}, bf16[64,2048]{1,0:T(8,128)(2,1)S(1)}, u32[]{:S(2)}, u32[]{:S(2)}) %collective-permute-start.4) | collective-permute-done | bytes 262176 | tf_op jit(solution)/shard_map/ppermute | solution.py:267
  167.7 5.0 %attend.8 = (f32[64,2048]{1,0:T(8,128)S(1)}, bf16[160,2048]{1,0:T(8,128)(2,1)}, f32[64,160]{1,0:T(8,128)S(1)}) custom-call(s32[1]{0:T(128)} %bitcast.segment, s32[2]{0:T(128)S(1)} %copy-done.20, bf16[64,2048]{1,0:T(8,128)(2,1)S(1)} %collective-permute-done.4.refs_0_, s32[2,64,2]{2,1,0:T(8,128)S(1)} %bitcast.100, bf16[32,2048]{1,0:T(8,128)(2,1)S(1)} %bitcast.82, ...), custom_call_target="tpu_custom_call" | custom-call | flops 805306368 | bytes 9437184 | tf_op jit(solution)/shard_map/attend/pallas_call | solution.py:114
  172.7 3.5 %all-to-all-start.7 = ((bf16[4,40,2048]{2,1,0:T(8,128)(2,1)}), bf16[4,40,2048]{2,1,0:T(8,128)(2,1)S(1)}, u32[]{:S(2)}, u32[]{:S(2)}) async-start(bf16[4,40,2048]{2,1,0:T(8,128)(2,1)} %bitcast.28), calls=%async_computation.7 | async-start | bytes 1310720 | tf_op jit(solution)/shard_map/all_to_all | solution.py:235
  176.3 7.3 %all-to-all-done.7 = bf16[4,40,2048]{2,1,0:T(8,128)(2,1)S(1)} async-done(((bf16[4,40,2048]{2,1,0:T(8,128)(2,1)}), bf16[4,40,2048]{2,1,0:T(8,128)(2,1)S(1)}, u32[]{:S(2)}, u32[]{:S(2)}) %all-to-all-start.7) | async-done | bytes 655392 | tf_op jit(solution)/shard_map/all_to_all | solution.py:235
  186.9 10.7 %experts.8 = bf16[160,2048]{1,0:T(8,128)(2,1)} custom-call(bf16[160,2048]{1,0:T(8,128)(2,1)S(1)} %bitcast.89, bf16[2048,2048]{1,0:T(8,128)(2,1)S(1)} %bitcast.67, bf16[2048,2048]{1,0:T(8,128)(2,1)} %bitcast.114, bf16[2048,2048]{1,0:T(8,128)(2,1)} %collective-permute-done.other_in, bf16[2048,2048]{1,0:T(8,128)(2,1)} %collective-permute-done.1.other_down), custom_call_target="tpu_custom_call" | custom-call | flops 5368709120 | bytes 34865152 | tf_op jit(solution)/shard_map/experts/pallas_call | solution.py:175
  197.6 3.5 %all-to-all-start.8 = ((bf16[4,40,2048]{2,1,0:T(8,128)(2,1)}), bf16[4,40,2048]{2,1,0:T(8,128)(2,1)S(1)}, u32[]{:S(2)}, u32[]{:S(2)}) async-start(bf16[4,40,2048]{2,1,0:T(8,128)(2,1)} %bitcast.30), calls=%async_computation.8 | async-start | bytes 1310720 | tf_op jit(solution)/shard_map/all_to_all | solution.py:235
  201.3 7.1 %all-to-all-done.8 = bf16[4,40,2048]{2,1,0:T(8,128)(2,1)S(1)} async-done(((bf16[4,40,2048]{2,1,0:T(8,128)(2,1)}), bf16[4,40,2048]{2,1,0:T(8,128)(2,1)S(1)}, u32[]{:S(2)}, u32[]{:S(2)}) %all-to-all-start.8) | async-done | bytes 655392 | tf_op jit(solution)/shard_map/all_to_all | solution.py:235
  208.8 4.6 %collective-permute-start.5 = (bf16[64,2048]{1,0:T(8,128)(2,1)S(1)}, bf16[64,2048]{1,0:T(8,128)(2,1)S(1)}, u32[]{:S(2)}, u32[]{:S(2)}) collective-permute-start(bf16[64,2048]{1,0:T(8,128)(2,1)S(1)} %combine.8), channel_id=1, source_target_pairs={{0,8},{8,16},{16,24},{1,9},{9,17},{17,25},{2,10},{10,18},{18,26},{... | collective-permute-start | bytes 786440 | tf_op jit(solution)/shard_map/ppermute | solution.py:267
  213.5 3.5 %collective-permute-done.5.refs_0_ = bf16[64,2048]{1,0:T(8,128)(2,1)S(1)} collective-permute-done((bf16[64,2048]{1,0:T(8,128)(2,1)S(1)}, bf16[64,2048]{1,0:T(8,128)(2,1)S(1)}, u32[]{:S(2)}, u32[]{:S(2)}) %collective-permute-start.5) | collective-permute-done | bytes 262176 | tf_op jit(solution)/shard_map/ppermute | solution.py:267
  221.4 5.0 %attend.9 = (f32[64,2048]{1,0:T(8,128)S(1)}, bf16[160,2048]{1,0:T(8,128)(2,1)}, f32[64,160]{1,0:T(8,128)S(1)}) custom-call(s32[1]{0:T(128)} %bitcast.segment, s32[2]{0:T(128)S(1)} %copy-done.21, bf16[64,2048]{1,0:T(8,128)(2,1)S(1)} %collective-permute-done.5.refs_0_, s32[2,64,2]{2,1,0:T(8,128)S(1)} %bitcast.101, bf16[32,2048]{1,0:T(8,128)(2,1)S(1)} %bitcast.83, ...), custom_call_target="tpu_custom_call" | custom-call | flops 805306368 | bytes 9437184 | tf_op jit(solution)/shard_map/attend/pallas_call | solution.py:114
  226.4 3.5 %all-to-all-start.9 = ((bf16[4,40,2048]{2,1,0:T(8,128)(2,1)}), bf16[4,40,2048]{2,1,0:T(8,128)(2,1)S(1)}, u32[]{:S(2)}, u32[]{:S(2)}) async-start(bf16[4,40,2048]{2,1,0:T(8,128)(2,1)} %bitcast.34), calls=%async_computation.9 | async-start | bytes 1310720 | tf_op jit(solution)/shard_map/all_to_all | solution.py:235
  230.0 7.2 %all-to-all-done.9 = bf16[4,40,2048]{2,1,0:T(8,128)(2,1)S(1)} async-done(((bf16[4,40,2048]{2,1,0:T(8,128)(2,1)}), bf16[4,40,2048]{2,1,0:T(8,128)(2,1)S(1)}, u32[]{:S(2)}, u32[]{:S(2)}) %all-to-all-start.9) | async-done | bytes 655392 | tf_op jit(solution)/shard_map/all_to_all | solution.py:235
  240.6 10.7 %experts.9 = bf16[160,2048]{1,0:T(8,128)(2,1)} custom-call(bf16[160,2048]{1,0:T(8,128)(2,1)S(1)} %bitcast.90, bf16[2048,2048]{1,0:T(8,128)(2,1)S(1)} %bitcast.68, bf16[2048,2048]{1,0:T(8,128)(2,1)} %bitcast.115, bf16[2048,2048]{1,0:T(8,128)(2,1)} %collective-permute-done.other_in, bf16[2048,2048]{1,0:T(8,128)(2,1)} %collective-permute-done.1.other_down), custom_call_target="tpu_custom_call" | custom-call | flops 5368709120 | bytes 34865152 | tf_op jit(solution)/shard_map/experts/pallas_call | solution.py:175
  254.9 7.2 %all-to-all-done.10 = bf16[4,40,2048]{2,1,0:T(8,128)(2,1)S(1)} async-done(((bf16[4,40,2048]{2,1,0:T(8,128)(2,1)}), bf16[4,40,2048]{2,1,0:T(8,128)(2,1)S(1)}, u32[]{:S(2)}, u32[]{:S(2)}) %all-to-all-start.10) | async-done | bytes 655392 | tf_op jit(solution)/shard_map/all_to_all | solution.py:235
  (74 shorter events, 41.1 us)
Async XLA Ops:
  0.0 0.7 copy-start
  0.0 44.2 %collective-permute-start = (bf16[2048,2048]{1,0:T(8,128)(2,1)}, bf16[2048,2048]{1,0:T(8,128)(2,1)}, u32[]{:S(2)}, u32[]{:S(2)}) collective-permute-start(bf16[2048,2048]{1,0:T(8,128)(2,1)} %bitcast.63), channel_id=1, source_target_pairs={{0,1},{1,0},{2,3},{3,2},{4,5},{5,4},{6,7},{7,6},{8,9},{9,8},{10,11... | collective-permute-start | bytes 25165832 | tf_op jit(solution)/shard_map/ppermute | solution.py:245
  0.5 43.7 %collective-permute-start.1 = (bf16[2048,2048]{1,0:T(8,128)(2,1)}, bf16[2048,2048]{1,0:T(8,128)(2,1)}, u32[]{:S(2)}, u32[]{:S(2)}) collective-permute-start(bf16[2048,2048]{1,0:T(8,128)(2,1)} %bitcast.110), channel_id=1, source_target_pairs={{0,1},{1,0},{2,3},{3,2},{4,5},{5,4},{6,7},{7,6},{8,9},{9,8},{10,11... | collective-permute-start | bytes 25165832 | tf_op jit(solution)/shard_map/ppermute | solution.py:245
  2.7 15.5 %all-to-all-start = ((bf16[32,2,1024]{2,1,0:T(2,128)(2,1)}), bf16[32,2,1024]{2,1,0:T(2,128)(2,1)S(1)}, u32[]{:S(2)}, u32[]{:S(2)}) async-start(bf16[32,2,1024]{2,1,0:T(2,128)(2,1)} %reshape.92), calls=%async_computation | async-start | bytes 262144 | tf_op jit(solution)/shard_map/all_to_all | solution.py:241
  18.3 25.9 %copy-start.1 = (bf16[1,1,2048,2048]{3,2,1,0:T(8,128)(2,1)S(1)}, bf16[1,1,2048,2048]{3,2,1,0:T(8,128)(2,1)}, u32[]{:S(2)}) copy-start(bf16[1,1,2048,2048]{3,2,1,0:T(8,128)(2,1)} %param.20) | copy-start | bytes 25165828
  18.4 2.3 copy-start.5
  20.7 2.5 copy-start.8
  23.2 1.1 copy-start.13
  24.3 0.7 copy-start.14
  25.0 0.7 copy-start.16
  44.2 27.4 %copy-start.6 = (bf16[1,2048,1024]{2,1,0:T(8,128)(2,1)S(1)}, bf16[1,2048,1024]{2,1,0:T(8,128)(2,1)}, u32[]{:S(2)}) copy-start(bf16[1,2048,1024]{2,1,0:T(8,128)(2,1)} %param.17) | copy-start | bytes 12582916
  66.4 5.2 %collective-permute-start.2 = (bf16[64,2048]{1,0:T(8,128)(2,1)S(1)}, bf16[64,2048]{1,0:T(8,128)(2,1)S(1)}, u32[]{:S(2)}, u32[]{:S(2)}) collective-permute-start(bf16[64,2048]{1,0:T(8,128)(2,1)S(1)} %combine.5), channel_id=1, source_target_pairs={{0,8},{8,16},{16,24},{1,9},{9,17},{17,25},{2,10},{10,18},{18,26},{... | collective-permute-start | bytes 786440 | tf_op jit(solution)/shard_map/ppermute | solution.py:267
  71.6 2.2 copy-start.9
  88.2 3.4 %copy-start.2 = (bf16[1,1,2048,2048]{3,2,1,0:T(8,128)(2,1)S(1)}, bf16[1,1,2048,2048]{3,2,1,0:T(8,128)(2,1)}, u32[]{:S(2)}) copy-start(bf16[1,1,2048,2048]{3,2,1,0:T(8,128)(2,1)} %param.20) | copy-start | bytes 25165828
  112.0 8.3 %collective-permute-start.3 = (bf16[64,2048]{1,0:T(8,128)(2,1)S(1)}, bf16[64,2048]{1,0:T(8,128)(2,1)S(1)}, u32[]{:S(2)}, u32[]{:S(2)}) collective-permute-start(bf16[64,2048]{1,0:T(8,128)(2,1)S(1)} %combine.6), channel_id=1, source_target_pairs={{0,8},{8,16},{16,24},{1,9},{9,17},{17,25},{2,10},{10,18},{18,26},{... | collective-permute-start | bytes 786440 | tf_op jit(solution)/shard_map/ppermute | solution.py:267
  120.3 2.2 copy-start.10
  157.3 8.3 %collective-permute-start.4 = (bf16[64,2048]{1,0:T(8,128)(2,1)S(1)}, bf16[64,2048]{1,0:T(8,128)(2,1)S(1)}, u32[]{:S(2)}, u32[]{:S(2)}) collective-permute-start(bf16[64,2048]{1,0:T(8,128)(2,1)S(1)} %combine.7), channel_id=1, source_target_pairs={{0,8},{8,16},{16,24},{1,9},{9,17},{17,25},{2,10},{10,18},{18,26},{... | collective-permute-start | bytes 786440 | tf_op jit(solution)/shard_map/ppermute | solution.py:267
  165.5 2.2 copy-start.11
  172.7 10.8 %all-to-all-start.7 = ((bf16[4,40,2048]{2,1,0:T(8,128)(2,1)}), bf16[4,40,2048]{2,1,0:T(8,128)(2,1)S(1)}, u32[]{:S(2)}, u32[]{:S(2)}) async-start(bf16[4,40,2048]{2,1,0:T(8,128)(2,1)} %bitcast.28), calls=%async_computation.7 | async-start | bytes 1310720 | tf_op jit(solution)/shard_map/all_to_all | solution.py:235
  183.5 3.4 %copy-start.3 = (bf16[1,1,2048,2048]{3,2,1,0:T(8,128)(2,1)S(1)}, bf16[1,1,2048,2048]{3,2,1,0:T(8,128)(2,1)}, u32[]{:S(2)}) copy-start(bf16[1,1,2048,2048]{3,2,1,0:T(8,128)(2,1)} %param.20) | copy-start | bytes 25165828
  186.9 30.1 %copy-start.15 = (bf16[1,2048,4]{1,2,0:T(4,128)(2,1)S(1)}, bf16[1,2048,4]{1,2,0:T(4,128)(2,1)}, u32[]{:S(2)}) copy-start(bf16[1,2048,4]{1,2,0:T(4,128)(2,1)} %param.19) | copy-start | bytes 49156
  186.9 30.1 %copy-start.17 = (f32[1,2048]{1,0:T(1,128)S(1)}, f32[1,2048]{1,0:T(1,128)}, u32[]{:S(2)}) copy-start(f32[1,2048]{1,0:T(1,128)} %refs_3_.7) | copy-start | bytes 24580
  186.9 30.1 %copy-start.19 = (f32[1,2048]{1,0:T(1,128)S(1)}, f32[1,2048]{1,0:T(1,128)}, u32[]{:S(2)}) copy-start(f32[1,2048]{1,0:T(1,128)} %refs_4_.9) | copy-start | bytes 24580
  186.9 30.1 %copy-start.21 = (s32[2]{0:T(128)S(1)}, s32[2]{0:T(128)}, u32[]{:S(2)}) copy-start(s32[2]{0:T(128)} %cand_len.9) | copy-start | bytes 28
  197.6 10.8 %all-to-all-start.8 = ((bf16[4,40,2048]{2,1,0:T(8,128)(2,1)}), bf16[4,40,2048]{2,1,0:T(8,128)(2,1)S(1)}, u32[]{:S(2)}, u32[]{:S(2)}) async-start(bf16[4,40,2048]{2,1,0:T(8,128)(2,1)} %bitcast.30), calls=%async_computation.8 | async-start | bytes 1310720 | tf_op jit(solution)/shard_map/all_to_all | solution.py:235
  208.8 8.2 %collective-permute-start.5 = (bf16[64,2048]{1,0:T(8,128)(2,1)S(1)}, bf16[64,2048]{1,0:T(8,128)(2,1)S(1)}, u32[]{:S(2)}, u32[]{:S(2)}) collective-permute-start(bf16[64,2048]{1,0:T(8,128)(2,1)S(1)} %combine.8), channel_id=1, source_target_pairs={{0,8},{8,16},{16,24},{1,9},{9,17},{17,25},{2,10},{10,18},{18,26},{... | collective-permute-start | bytes 786440 | tf_op jit(solution)/shard_map/ppermute | solution.py:267
  217.0 2.2 copy-start.7
  219.2 2.2 copy-start.12
  226.4 10.8 %all-to-all-start.9 = ((bf16[4,40,2048]{2,1,0:T(8,128)(2,1)}), bf16[4,40,2048]{2,1,0:T(8,128)(2,1)S(1)}, u32[]{:S(2)}, u32[]{:S(2)}) async-start(bf16[4,40,2048]{2,1,0:T(8,128)(2,1)} %bitcast.34), calls=%async_computation.9 | async-start | bytes 1310720 | tf_op jit(solution)/shard_map/all_to_all | solution.py:235
  237.2 3.4 %copy-start.4 = (bf16[1,1,2048,2048]{3,2,1,0:T(8,128)(2,1)S(1)}, bf16[1,1,2048,2048]{3,2,1,0:T(8,128)(2,1)}, u32[]{:S(2)}) copy-start(bf16[1,1,2048,2048]{3,2,1,0:T(8,128)(2,1)} %param.20) | copy-start | bytes 25165828
  251.3 10.8 %all-to-all-start.10 = ((bf16[4,40,2048]{2,1,0:T(8,128)(2,1)}), bf16[4,40,2048]{2,1,0:T(8,128)(2,1)S(1)}, u32[]{:S(2)}, u32[]{:S(2)}) async-start(bf16[4,40,2048]{2,1,0:T(8,128)(2,1)} %bitcast.36), calls=%async_computation.10 | async-start | bytes 1310720 | tf_op jit(solution)/shard_map/all_to_all | solution.py:235
  262.5 0.8 copy-start.22
  (2 other events, 1.4 us)

commit v2 on v1

--- a/solution.py
+++ b/solution.py
@@ -18,9 +18,13 @@
 
 VMEM = pl.BlockSpec(memory_space=pltpu.VMEM)
 SMEM = pl.BlockSpec(memory_space=pltpu.SMEM)
-ANY = pl.BlockSpec(memory_space=pl.ANY)
+HBM = pl.BlockSpec(memory_space=pltpu.HBM)
 F32 = jnp.float32
 BF16 = jnp.bfloat16
+
+
+def in_hbm(*arrays):
+    return [pltpu.with_memory_space_constraint(array, pltpu.HBM) for array in arrays]
 
 
 def normalize(carried, gain_row):
@@ -34,31 +38,43 @@
     return lax.dot_general(left, right, (contract, ((), ())), preferred_element_type=F32)
 
 
-def attend_kernel(
-    step, capacity, segment, cand_len, *refs
-):
-    if step == 0:
-        fresh, refs = refs[0], refs[1:]
-    elif step == 1:
-        fresh, incoming, refs = refs[0], refs[1], refs[2:]
-    else:
+def attend_kernel(step, capacity, scalars, *refs):
+    incoming = states = None
+    if step > 0:
         incoming, refs = refs[0], refs[1:]
+    if step < CAND_DEV:
+        states, refs = refs[0], refs[1:]
     (routes, cached, attn_gain, ffn_gain, w_query, w_out, router_t,
-     after_ref, outgoing, weights, query_buf, out_buf, context, sems) = refs
-    query_copy = pltpu.make_async_copy(w_query, query_buf, sems.at[0])
-    out_copy = pltpu.make_async_copy(w_out, out_buf, sems.at[1])
-    query_copy.start()
-    out_copy.start()
+     after_ref, outgoing, weights,
+     fresh, gain_buf, router_buf, query_buf, out_buf, context, sems) = refs
+    segment = scalars[0]
+    fills = [
+        (attn_gain, gain_buf.at[0]),
+        (ffn_gain, gain_buf.at[1]),
+        (w_query, query_buf),
+        (w_out, out_buf),
+        (router_t, router_buf),
+    ]
+    if states is not None:
+        fills.insert(0, (states.at[pl.ds(step * CAND_LEN, CAND_LEN), :], fresh))
+    copies = [pltpu.make_async_copy(*pair, sems.at[i]) for i, pair in enumerate(fills)]
+    for copy in copies:
+        copy.start()
+    if states is not None:
+        copies[0].wait()
+        copies = copies[1:]
 
     if step == 0:
         current = fresh[...]
-    elif step == 1:
-        current = jnp.where(segment[0] == 0, fresh[...], incoming[...])
+    elif step < CAND_DEV:
+        current = jnp.where(segment == 0, fresh[...], incoming[...])
     else:
         current = incoming[...]
+    copies[0].wait()
+    copies[1].wait()
     carried = current.astype(F32)
-    normed = normalize(carried, attn_gain[...]).astype(BF16)
-    query_copy.wait()
+    normed = normalize(carried, gain_buf[0]).astype(BF16)
+    copies[2].wait()
     queries = dot(normed, query_buf[...]).astype(BF16)
     head_total = queries.shape[1]
     scale = 1.0 / math.sqrt(HEAD_DIM)
@@ -69,15 +85,16 @@
         share = (exponent / jnp.sum(exponent, axis=1, keepdims=True)).astype(BF16)
         values = cached[:, head_total + start : head_total + start + HEAD_DIM]
         context[:, lanes] = dot(share, values).astype(BF16)
-    out_copy.wait()
+    copies[3].wait()
     after_attn = carried + dot(context[...], out_buf[...])
     after_ref[...] = after_attn
-    ffn_input = normalize(after_attn, ffn_gain[...]).astype(BF16)
+    ffn_input = normalize(after_attn, gain_buf[1]).astype(BF16)
 
     rows, experts = after_attn.shape[0], router_t.shape[0]
-    logits = dot(ffn_input, router_t[...], ((1,), (1,)))
-    micro = jnp.clip(step - segment[0], 0, CAND_DEV - 1)
-    live = lax.broadcasted_iota(jnp.int32, (rows, 1), 0) < cand_len[micro]
+    copies[4].wait()
+    logits = dot(ffn_input, router_buf[...], ((1,), (1,)))
+    micro = jnp.clip(step - segment, 0, CAND_DEV - 1)
+    live = lax.broadcasted_iota(jnp.int32, (rows, 1), 0) < scalars[1 + micro]
     route = routes[micro]
     labels = lax.broadcasted_iota(jnp.int32, (rows, experts), 1)
     first, second = route[:, 0:1] == labels, route[:, 1:2] == labels
@@ -101,20 +118,20 @@
     weights[...] = jnp.where(chosen[0], gate_first, 0.0) + jnp.where(chosen[1], gate_second, 0.0)
 
 
-def attend(step, capacity, segment, cand_len, sources, routes, cached, gains, mats):
+def attend(step, capacity, scalars, states, incoming, routes, cached, gains, mats):
     w_query, w_out, router_t = mats
     width, head_total = w_query.shape
     slot_count = router_t.shape[0] * capacity
-    specs = [SMEM, SMEM]
-    for source in sources:
-        if source.shape[0] == CAND_LEN:
-            specs.append(VMEM)
-        else:
-            specs.append(pl.BlockSpec((CAND_LEN, width), lambda i: (min(step, CAND_DEV - 1), 0)))
+    sources, specs = [], []
+    if step > 0:
+        sources.append(incoming)
+        specs.append(VMEM)
+    if step < CAND_DEV:
+        sources += in_hbm(states)
+        specs.append(HBM)
     return pl.pallas_call(
         functools.partial(attend_kernel, step, capacity),
-        grid=(1,),
-        in_specs=specs + [VMEM, VMEM, VMEM, VMEM, ANY, ANY, VMEM],
+        in_specs=[SMEM] + specs + [VMEM, VMEM, HBM, HBM, HBM, HBM, HBM],
         out_specs=[VMEM, VMEM, VMEM],
         out_shape=[
             jax.ShapeDtypeStruct((CAND_LEN, width), F32),
@@ -122,10 +139,13 @@
             jax.ShapeDtypeStruct((CAND_LEN, slot_count), F32),
         ],
         scratch_shapes=[
+            pltpu.VMEM((CAND_LEN, width), BF16),
+            pltpu.VMEM((2, 1, width), F32),
+            pltpu.VMEM(router_t.shape, BF16),
             pltpu.VMEM(w_query.shape, BF16),
             pltpu.VMEM(w_out.shape, BF16),
             pltpu.VMEM((CAND_LEN, head_total), BF16),
-            pltpu.SemaphoreType.DMA((2,)),
+            pltpu.SemaphoreType.DMA((6,)),
         ],
         compiler_params=pltpu.CompilerParams(vmem_limit_bytes=24 * MIB),
         cost_estimate=pl.CostEstimate(
@@ -134,7 +154,7 @@
             transcendentals=0,
         ),
         name="attend",
-    )(segment, cand_len, *sources, routes, cached, *gains, w_query, w_out, router_t)
+    )(scalars, *sources, routes, cached, *in_hbm(*gains, w_query, w_out, router_t))
 
 
 def expert_kernel(rows, own_in, own_down, other_in, other_down, served, in_buf, down_buf, total, in_sems, down_sems):
@@ -174,7 +194,7 @@
     chunks = 2 * units // HIDDEN_CHUNK
     return pl.pallas_call(
         expert_kernel,
-        in_specs=[VMEM, ANY, ANY, ANY, ANY],
+        in_specs=[VMEM, HBM, HBM, HBM, HBM],
         out_specs=VMEM,
         out_shape=jax.ShapeDtypeStruct(rows.shape, BF16),
         scratch_shapes=[
@@ -191,7 +211,7 @@
             transcendentals=0,
         ),
         name="experts",
-    )(rows, own_in, own_down, other_in, other_down)
+    )(rows, *in_hbm(own_in, own_down, other_in, other_down))
 
 
 def combine_kernel(after_attn, weights, expert_out, result):
@@ -244,21 +264,15 @@
     own = (w_in[0, 0], w_down[0, 0])
     other = tuple(lax.ppermute(mat, "expert", core_pairs) for mat in own)
 
-    segment = segment_index.astype(jnp.int32).reshape(1)
+    scalars = jnp.concatenate([segment_index.astype(jnp.int32).reshape(1), cand_len])
     route_all = routes[0].reshape(CAND_DEV, CAND_LEN, 2)
     mats = (w_query[0], w_out[0], w_router[0].T)
     outputs = jnp.zeros((CAND_DEV, CAND_LEN, model_width), BF16)
     step_count = CAND_DEV + n_segment - 1
     incoming = None
     for step in range(step_count):
-        if step == 0:
-            sources = (states,)
-        elif step < CAND_DEV:
-            sources = (states, incoming)
-        else:
-            sources = (incoming,)
         after_attn, outgoing, weights = attend(
-            step, capacity, segment, cand_len, sources, route_all, cached,
+            step, capacity, scalars, states, incoming, route_all, cached,
             (attn_gain, ffn_gain), mats,
         )
         served = expert_rows(exchange(outgoing), *own, *other)

time: 265 us -> 252 us (0.951)
  local copies, waits for them, and re-layouts: 33.1 us -> 3.36 us
  Pallas kernels: 75.3 us -> 92.5 us
    unnamed x50 -> x8, local copies, waits for them, and re-layouts: 32.4 us -> 2.68 us
    pallas_call x10, Pallas kernels: 73.6 us -> 90.8 us  [the longest x5 59.1 us: expert_rows(): pl.pallas_call(expert_kernel, in_specs=[VMEM, HBM, HBM, HBM, HBM], out_sp...]
  transfers between devices with their start and end apart: 11 -> 11, of which waited for: 9 -> 9; matrix products, arithmetic and copies ran while one was open for 1% -> 2% of each run, Pallas kernels for 2% -> 2%
where the time goes in v2:
time: 252 us; the launch traced here: 251 us
  Pallas kernels  92.5 us (37%)
  blocking collectives  65.8 us (26%)
  waiting for transfers between devices  50.8 us (20%)
  starting transfers between devices  36.3 us (14%)
  local copies, waits for them, and re-layouts  3.36 us (1%)
    all_to_all x6, blocking collectives, exchange(): lax.all_to_all(blocks, 'expert', split_axis=0, concat_axis=0, axis_index_...  65.8 us
    pallas_call x5, Pallas kernels, expert_rows(): pl.pallas_call(expert_kernel, in_specs=[VMEM, HBM, HBM, HBM, HBM], out_sp...  59.1 us
    pallas_call x5, Pallas kernels, attend(): pl.pallas_call(functools.partial(attend_kernel, step, capacity), in_specs...  31.7 us
    all_to_all x4, waiting for transfers between devices, exchange(): lax.all_to_all(blocks, 'expert', split_axis=0, concat_axis=0, axis_index_...  28.8 us
    ppermute x4, waiting for transfers between devices, local(): lax.ppermute(result, 'segment', [(i, i + 1) for i in range(n_segment - 1)])  15.3 us
    ppermute x4, starting transfers between devices, local(): lax.ppermute(result, 'segment', [(i, i + 1) for i in range(n_segment - 1)])  14.5 us
    all_to_all x4, starting transfers between devices, exchange(): lax.all_to_all(blocks, 'expert', split_axis=0, concat_axis=0, axis_index_...  14 us
    all_to_all x1, starting transfers between devices, local(): lax.all_to_all(spread, ('segment', 'expert'), split_axis=0, concat_axis=0...  7.3 us
  transfers between devices with their start and end apart: 11, of which 9 were waited for; matrix products, arithmetic and copies ran while one was open for 2% of the time, Pallas kernels for 2%

profile of v2, /device:TPU:0, one launch (start us, length us, event | category | flops | bytes accessed | tf_op | source)
XLA Modules:
  0.0 250.8 jit_solution(16692896215051494855)
XLA Ops:
  2.7 7.3 %all-to-all-start = ((bf16[32,2,1024]{2,1,0:T(2,128)(2,1)}), bf16[32,2,1024]{2,1,0:T(2,128)(2,1)S(1)}, u32[]{:S(2)}, u32[]{:S(2)}) async-start(bf16[32,2,1024]{2,1,0:T(2,128)(2,1)} %reshape.92), calls=%async_computation | async-start | bytes 262144 | tf_op jit(solution)/shard_map/all_to_all | solution.py:261
  11.5 6.7 %all-to-all-done = bf16[32,2,1024]{2,1,0:T(2,128)(2,1)S(1)} async-done(((bf16[32,2,1024]{2,1,0:T(2,128)(2,1)}), bf16[32,2,1024]{2,1,0:T(2,128)(2,1)S(1)}, u32[]{:S(2)}, u32[]{:S(2)}) %all-to-all-start) | async-done | bytes 131104 | tf_op jit(solution)/shard_map/all_to_all | solution.py:261
  18.4 6.1 %attend.5 = (f32[64,2048]{1,0:T(8,128)S(1)}, bf16[160,2048]{1,0:T(8,128)(2,1)S(1)}, f32[64,160]{1,0:T(8,128)S(1)}) custom-call(s32[3]{0:T(128)S(1)} %pad_add_fusion.scalars, bf16[128,2048]{1,0:T(8,128)(2,1)} %refs_1_.1, s32[2,64,2]{2,1,0:T(8,128)S(1)} %bitcast.81, bf16[32,2048]{1,0:T(8,128)(2,1)S(1)} %bitcast.63, f32[1,2048]{1,0:T(1,128)} %refs_3_.7, ...), custom_call_target="tpu_custom_call" | custom-call | flops 805306368 | bytes 9437184 | tf_op jit(solution)/shard_map/attend/pallas_call | solution.py:132
  24.5 13.0 %all_to_all.61 = bf16[4,40,2048]{2,1,0:T(8,128)(2,1)S(1)} all-to-all(bf16[4,40,2048]{2,1,0:T(8,128)(2,1)S(1)} %bitcast.88), channel_id=1, replica_groups={{0,2,4,6},{1,3,5,7},{8,10,12,14},{9,11,13,15},{16,18,20,22},{17,19,21,2..., dimensions={0} | all-to-all | bytes 1310720 | tf_op jit(solution)/shard_map/all_to_all | solution.py:255
  37.5 11.5 %experts.5 = bf16[160,2048]{1,0:T(8,128)(2,1)S(1)} custom-call(bf16[160,2048]{1,0:T(8,128)(2,1)S(1)} %bitcast.75, bf16[2048,2048]{1,0:T(8,128)(2,1)} %bitcast.90, bf16[2048,2048]{1,0:T(8,128)(2,1)} %bitcast.96, bf16[2048,2048]{1,0:T(8,128)(2,1)} %collective-permute-done.other_in, bf16[2048,2048]{1,0:T(8,128)(2,1)} %collective-permute-done.1.other_down), custom_call_target="tpu_custom_call" | custom-call | flops 5368709120 | bytes 34865152 | tf_op jit(solution)/shard_map/experts/pallas_call | solution.py:195
  49.0 11.8 %all_to_all.62 = bf16[4,40,2048]{2,1,0:T(8,128)(2,1)S(1)} all-to-all(bf16[4,40,2048]{2,1,0:T(8,128)(2,1)S(1)} %bitcast.76), channel_id=1, replica_groups={{0,2,4,6},{1,3,5,7},{8,10,12,14},{9,11,13,15},{16,18,20,22},{17,19,21,2..., dimensions={0} | all-to-all | bytes 1310720 | tf_op jit(solution)/shard_map/all_to_all | solution.py:255
  62.4 3.9 %collective-permute-done.2.refs_0_ = bf16[64,2048]{1,0:T(8,128)(2,1)S(1)} collective-permute-done((bf16[64,2048]{1,0:T(8,128)(2,1)S(1)}, bf16[64,2048]{1,0:T(8,128)(2,1)S(1)}, u32[]{:S(2)}, u32[]{:S(2)}) %collective-permute-start.2) | collective-permute-done | bytes 262176 | tf_op jit(solution)/shard_map/ppermute | solution.py:281
  66.3 6.1 %attend.6 = (f32[64,2048]{1,0:T(8,128)S(1)}, bf16[160,2048]{1,0:T(8,128)(2,1)S(1)}, f32[64,160]{1,0:T(8,128)S(1)}) custom-call(s32[3]{0:T(128)S(1)} %pad_add_fusion.scalars, bf16[64,2048]{1,0:T(8,128)(2,1)S(1)} %collective-permute-done.2.refs_0_, bf16[128,2048]{1,0:T(8,128)(2,1)} %refs_1_.1, s32[2,64,2]{2,1,0:T(8,128)S(1)} %bitcast.82, ...), custom_call_target="tpu_custom_call" | custom-call | flops 805306368 | bytes 9437184 | tf_op jit(solution)/shard_map/attend/pallas_call | solution.py:132
  72.4 10.2 %all_to_all.63 = bf16[4,40,2048]{2,1,0:T(8,128)(2,1)S(1)} all-to-all(bf16[4,40,2048]{2,1,0:T(8,128)(2,1)S(1)} %bitcast.86), channel_id=1, replica_groups={{0,2,4,6},{1,3,5,7},{8,10,12,14},{9,11,13,15},{16,18,20,22},{17,19,21,2..., dimensions={0} | all-to-all | bytes 1310720 | tf_op jit(solution)/shard_map/all_to_all | solution.py:255
  82.6 11.5 %experts.6 = bf16[160,2048]{1,0:T(8,128)(2,1)S(1)} custom-call(bf16[160,2048]{1,0:T(8,128)(2,1)S(1)} %bitcast.77, bf16[2048,2048]{1,0:T(8,128)(2,1)} %bitcast.91, bf16[2048,2048]{1,0:T(8,128)(2,1)} %bitcast.97, bf16[2048,2048]{1,0:T(8,128)(2,1)} %collective-permute-done.other_in, bf16[2048,2048]{1,0:T(8,128)(2,1)} %collective-permute-done.1.other_down), custom_call_target="tpu_custom_call" | custom-call | flops 5368709120 | bytes 34865152 | tf_op jit(solution)/shard_map/experts/pallas_call | solution.py:195
  94.1 10.2 %all_to_all.64 = bf16[4,40,2048]{2,1,0:T(8,128)(2,1)S(1)} all-to-all(bf16[4,40,2048]{2,1,0:T(8,128)(2,1)S(1)} %bitcast.78), channel_id=1, replica_groups={{0,2,4,6},{1,3,5,7},{8,10,12,14},{9,11,13,15},{16,18,20,22},{17,19,21,2..., dimensions={0} | all-to-all | bytes 1310720 | tf_op jit(solution)/shard_map/all_to_all | solution.py:255
  104.7 4.4 %collective-permute-start.3 = (bf16[64,2048]{1,0:T(8,128)(2,1)S(1)}, bf16[64,2048]{1,0:T(8,128)(2,1)S(1)}, u32[]{:S(2)}, u32[]{:S(2)}) collective-permute-start(bf16[64,2048]{1,0:T(8,128)(2,1)S(1)} %combine.6), channel_id=1, source_target_pairs={{0,8},{8,16},{16,24},{1,9},{9,17},{17,25},{2,10},{10,18},{18,26},{... | collective-permute-start | bytes 786440 | tf_op jit(solution)/shard_map/ppermute | solution.py:281
  109.1 3.9 %collective-permute-done.3.refs_0_ = bf16[64,2048]{1,0:T(8,128)(2,1)S(1)} collective-permute-done((bf16[64,2048]{1,0:T(8,128)(2,1)S(1)}, bf16[64,2048]{1,0:T(8,128)(2,1)S(1)}, u32[]{:S(2)}, u32[]{:S(2)}) %collective-permute-start.3) | collective-permute-done | bytes 262176 | tf_op jit(solution)/shard_map/ppermute | solution.py:281
  112.9 6.0 %attend.7 = (f32[64,2048]{1,0:T(8,128)S(1)}, bf16[160,2048]{1,0:T(8,128)(2,1)S(1)}, f32[64,160]{1,0:T(8,128)S(1)}) custom-call(s32[3]{0:T(128)S(1)} %pad_add_fusion.scalars, bf16[64,2048]{1,0:T(8,128)(2,1)S(1)} %collective-permute-done.3.refs_0_, s32[2,64,2]{2,1,0:T(8,128)S(1)} %bitcast.83, bf16[32,2048]{1,0:T(8,128)(2,1)S(1)} %bitcast.65, ...), custom_call_target="tpu_custom_call" | custom-call | flops 805306368 | bytes 9437184 | tf_op jit(solution)/shard_map/attend/pallas_call | solution.py:132
  118.9 10.2 %all_to_all.65 = bf16[4,40,2048]{2,1,0:T(8,128)(2,1)S(1)} all-to-all(bf16[4,40,2048]{2,1,0:T(8,128)(2,1)S(1)} %bitcast.87), channel_id=1, replica_groups={{0,2,4,6},{1,3,5,7},{8,10,12,14},{9,11,13,15},{16,18,20,22},{17,19,21,2..., dimensions={0} | all-to-all | bytes 1310720 | tf_op jit(solution)/shard_map/all_to_all | solution.py:255
  129.2 11.5 %experts.7 = bf16[160,2048]{1,0:T(8,128)(2,1)S(1)} custom-call(bf16[160,2048]{1,0:T(8,128)(2,1)S(1)} %bitcast.79, bf16[2048,2048]{1,0:T(8,128)(2,1)} %bitcast.92, bf16[2048,2048]{1,0:T(8,128)(2,1)} %bitcast.98, bf16[2048,2048]{1,0:T(8,128)(2,1)} %collective-permute-done.other_in, bf16[2048,2048]{1,0:T(8,128)(2,1)} %collective-permute-done.1.other_down), custom_call_target="tpu_custom_call" | custom-call | flops 5368709120 | bytes 34865152 | tf_op jit(solution)/shard_map/experts/pallas_call | solution.py:195
  140.6 10.2 %all_to_all.66 = bf16[4,40,2048]{2,1,0:T(8,128)(2,1)S(1)} all-to-all(bf16[4,40,2048]{2,1,0:T(8,128)(2,1)S(1)} %bitcast.80), channel_id=1, replica_groups={{0,2,4,6},{1,3,5,7},{8,10,12,14},{9,11,13,15},{16,18,20,22},{17,19,21,2..., dimensions={0} | all-to-all | bytes 1310720 | tf_op jit(solution)/shard_map/all_to_all | solution.py:255
  151.2 4.4 %collective-permute-start.4 = (bf16[64,2048]{1,0:T(8,128)(2,1)S(1)}, bf16[64,2048]{1,0:T(8,128)(2,1)S(1)}, u32[]{:S(2)}, u32[]{:S(2)}) collective-permute-start(bf16[64,2048]{1,0:T(8,128)(2,1)S(1)} %combine.7), channel_id=1, source_target_pairs={{0,8},{8,16},{16,24},{1,9},{9,17},{17,25},{2,10},{10,18},{18,26},{... | collective-permute-start | bytes 786440 | tf_op jit(solution)/shard_map/ppermute | solution.py:281
  155.6 3.9 %collective-permute-done.4.refs_0_ = bf16[64,2048]{1,0:T(8,128)(2,1)S(1)} collective-permute-done((bf16[64,2048]{1,0:T(8,128)(2,1)S(1)}, bf16[64,2048]{1,0:T(8,128)(2,1)S(1)}, u32[]{:S(2)}, u32[]{:S(2)}) %collective-permute-start.4) | collective-permute-done | bytes 262176 | tf_op jit(solution)/shard_map/ppermute | solution.py:281
  159.5 6.8 %attend.8 = (f32[64,2048]{1,0:T(8,128)S(1)}, bf16[160,2048]{1,0:T(8,128)(2,1)}, f32[64,160]{1,0:T(8,128)S(1)}) custom-call(s32[3]{0:T(128)S(1)} %pad_add_fusion.scalars, bf16[64,2048]{1,0:T(8,128)(2,1)S(1)} %collective-permute-done.4.refs_0_, s32[2,64,2]{2,1,0:T(8,128)S(1)} %bitcast.84, bf16[32,2048]{1,0:T(8,128)(2,1)S(1)} %bitcast.66, f32[1,2048]{1,0:T(1,128)} %refs_3_.7, ...), custom_call_target="tpu_custom_call" | custom-call | flops 805306368 | bytes 9437184 | tf_op jit(solution)/shard_map/attend/pallas_call | solution.py:132
  166.3 3.5 %all-to-all-start.7 = ((bf16[4,40,2048]{2,1,0:T(8,128)(2,1)}), bf16[4,40,2048]{2,1,0:T(8,128)(2,1)S(1)}, u32[]{:S(2)}, u32[]{:S(2)}) async-start(bf16[4,40,2048]{2,1,0:T(8,128)(2,1)} %bitcast.28), calls=%async_computation.7 | async-start | bytes 1310720 | tf_op jit(solution)/shard_map/all_to_all | solution.py:255
  169.9 7.3 %all-to-all-done.7 = bf16[4,40,2048]{2,1,0:T(8,128)(2,1)S(1)} async-done(((bf16[4,40,2048]{2,1,0:T(8,128)(2,1)}), bf16[4,40,2048]{2,1,0:T(8,128)(2,1)S(1)}, u32[]{:S(2)}, u32[]{:S(2)}) %all-to-all-start.7) | async-done | bytes 655392 | tf_op jit(solution)/shard_map/all_to_all | solution.py:255
  177.1 12.3 %experts.8 = bf16[160,2048]{1,0:T(8,128)(2,1)} custom-call(bf16[160,2048]{1,0:T(8,128)(2,1)S(1)} %bitcast.73, bf16[2048,2048]{1,0:T(8,128)(2,1)} %bitcast.93, bf16[2048,2048]{1,0:T(8,128)(2,1)} %bitcast.99, bf16[2048,2048]{1,0:T(8,128)(2,1)} %collective-permute-done.other_in, bf16[2048,2048]{1,0:T(8,128)(2,1)} %collective-permute-done.1.other_down), custom_call_target="tpu_custom_call" | custom-call | flops 5368709120 | bytes 34865152 | tf_op jit(solution)/shard_map/experts/pallas_call | solution.py:195
  189.4 3.5 %all-to-all-start.8 = ((bf16[4,40,2048]{2,1,0:T(8,128)(2,1)}), bf16[4,40,2048]{2,1,0:T(8,128)(2,1)S(1)}, u32[]{:S(2)}, u32[]{:S(2)}) async-start(bf16[4,40,2048]{2,1,0:T(8,128)(2,1)} %bitcast.30), calls=%async_computation.8 | async-start | bytes 1310720 | tf_op jit(solution)/shard_map/all_to_all | solution.py:255
  193.1 7.1 %all-to-all-done.8 = bf16[4,40,2048]{2,1,0:T(8,128)(2,1)S(1)} async-done(((bf16[4,40,2048]{2,1,0:T(8,128)(2,1)}), bf16[4,40,2048]{2,1,0:T(8,128)(2,1)S(1)}, u32[]{:S(2)}, u32[]{:S(2)}) %all-to-all-start.8) | async-done | bytes 655392 | tf_op jit(solution)/shard_map/all_to_all | solution.py:255
  200.6 4.4 %collective-permute-start.5 = (bf16[64,2048]{1,0:T(8,128)(2,1)S(1)}, bf16[64,2048]{1,0:T(8,128)(2,1)S(1)}, u32[]{:S(2)}, u32[]{:S(2)}) collective-permute-start(bf16[64,2048]{1,0:T(8,128)(2,1)S(1)} %combine.8), channel_id=1, source_target_pairs={{0,8},{8,16},{16,24},{1,9},{9,17},{17,25},{2,10},{10,18},{18,26},{... | collective-permute-start | bytes 786440 | tf_op jit(solution)/shard_map/ppermute | solution.py:281
  205.1 3.7 %collective-permute-done.5.refs_0_ = bf16[64,2048]{1,0:T(8,128)(2,1)S(1)} collective-permute-done((bf16[64,2048]{1,0:T(8,128)(2,1)S(1)}, bf16[64,2048]{1,0:T(8,128)(2,1)S(1)}, u32[]{:S(2)}, u32[]{:S(2)}) %collective-permute-start.5) | collective-permute-done | bytes 262176 | tf_op jit(solution)/shard_map/ppermute | solution.py:281
  208.9 6.8 %attend.9 = (f32[64,2048]{1,0:T(8,128)S(1)}, bf16[160,2048]{1,0:T(8,128)(2,1)}, f32[64,160]{1,0:T(8,128)S(1)}) custom-call(s32[3]{0:T(128)S(1)} %pad_add_fusion.scalars, bf16[64,2048]{1,0:T(8,128)(2,1)S(1)} %collective-permute-done.5.refs_0_, s32[2,64,2]{2,1,0:T(8,128)S(1)} %bitcast.85, bf16[32,2048]{1,0:T(8,128)(2,1)S(1)} %bitcast.67, f32[1,2048]{1,0:T(1,128)} %refs_3_.7, ...), custom_call_target="tpu_custom_call" | custom-call | flops 805306368 | bytes 9437184 | tf_op jit(solution)/shard_map/attend/pallas_call | solution.py:132
  215.7 3.5 %all-to-all-start.9 = ((bf16[4,40,2048]{2,1,0:T(8,128)(2,1)}), bf16[4,40,2048]{2,1,0:T(8,128)(2,1)S(1)}, u32[]{:S(2)}, u32[]{:S(2)}) async-start(bf16[4,40,2048]{2,1,0:T(8,128)(2,1)} %bitcast.34), calls=%async_computation.9 | async-start | bytes 1310720 | tf_op jit(solution)/shard_map/all_to_all | solution.py:255
  219.3 7.2 %all-to-all-done.9 = bf16[4,40,2048]{2,1,0:T(8,128)(2,1)S(1)} async-done(((bf16[4,40,2048]{2,1,0:T(8,128)(2,1)}), bf16[4,40,2048]{2,1,0:T(8,128)(2,1)S(1)}, u32[]{:S(2)}, u32[]{:S(2)}) %all-to-all-start.9) | async-done | bytes 655392 | tf_op jit(solution)/shard_map/all_to_all | solution.py:255
  226.5 12.3 %experts.9 = bf16[160,2048]{1,0:T(8,128)(2,1)} custom-call(bf16[160,2048]{1,0:T(8,128)(2,1)S(1)} %bitcast.74, bf16[2048,2048]{1,0:T(8,128)(2,1)} %bitcast.94, bf16[2048,2048]{1,0:T(8,128)(2,1)} %bitcast.100, bf16[2048,2048]{1,0:T(8,128)(2,1)} %collective-permute-done.other_in, bf16[2048,2048]{1,0:T(8,128)(2,1)} %collective-permute-done.1.other_down), custom_call_target="tpu_custom_call" | custom-call | flops 5368709120 | bytes 34865152 | tf_op jit(solution)/shard_map/experts/pallas_call | solution.py:195
  242.4 7.2 %all-to-all-done.10 = bf16[4,40,2048]{2,1,0:T(8,128)(2,1)S(1)} async-done(((bf16[4,40,2048]{2,1,0:T(8,128)(2,1)}), bf16[4,40,2048]{2,1,0:T(8,128)(2,1)S(1)}, u32[]{:S(2)}, u32[]{:S(2)}) %all-to-all-start.10) | async-done | bytes 655392 | tf_op jit(solution)/shard_map/all_to_all | solution.py:255
  (33 shorter events, 12.1 us)
Async XLA Ops:
  0.0 0.7 copy-start
  0.0 37.5 %collective-permute-start = (bf16[2048,2048]{1,0:T(8,128)(2,1)}, bf16[2048,2048]{1,0:T(8,128)(2,1)}, u32[]{:S(2)}, u32[]{:S(2)}) collective-permute-start(bf16[2048,2048]{1,0:T(8,128)(2,1)} %bitcast.89), channel_id=1, source_target_pairs={{0,1},{1,0},{2,3},{3,2},{4,5},{5,4},{6,7},{7,6},{8,9},{9,8},{10,11... | collective-permute-start | bytes 25165832 | tf_op jit(solution)/shard_map/ppermute | solution.py:265
  0.5 37.0 %collective-permute-start.1 = (bf16[2048,2048]{1,0:T(8,128)(2,1)}, bf16[2048,2048]{1,0:T(8,128)(2,1)}, u32[]{:S(2)}, u32[]{:S(2)}) collective-permute-start(bf16[2048,2048]{1,0:T(8,128)(2,1)} %bitcast.95), channel_id=1, source_target_pairs={{0,1},{1,0},{2,3},{3,2},{4,5},{5,4},{6,7},{7,6},{8,9},{9,8},{10,11... | collective-permute-start | bytes 25165832 | tf_op jit(solution)/shard_map/ppermute | solution.py:265
  2.7 15.5 %all-to-all-start = ((bf16[32,2,1024]{2,1,0:T(2,128)(2,1)}), bf16[32,2,1024]{2,1,0:T(2,128)(2,1)S(1)}, u32[]{:S(2)}, u32[]{:S(2)}) async-start(bf16[32,2,1024]{2,1,0:T(2,128)(2,1)} %reshape.92), calls=%async_computation | async-start | bytes 262144 | tf_op jit(solution)/shard_map/all_to_all | solution.py:261
  61.1 5.2 %collective-permute-start.2 = (bf16[64,2048]{1,0:T(8,128)(2,1)S(1)}, bf16[64,2048]{1,0:T(8,128)(2,1)S(1)}, u32[]{:S(2)}, u32[]{:S(2)}) collective-permute-start(bf16[64,2048]{1,0:T(8,128)(2,1)S(1)} %combine.5), channel_id=1, source_target_pairs={{0,8},{8,16},{16,24},{1,9},{9,17},{17,25},{2,10},{10,18},{18,26},{... | collective-permute-start | bytes 786440 | tf_op jit(solution)/shard_map/ppermute | solution.py:281
  104.7 8.3 %collective-permute-start.3 = (bf16[64,2048]{1,0:T(8,128)(2,1)S(1)}, bf16[64,2048]{1,0:T(8,128)(2,1)S(1)}, u32[]{:S(2)}, u32[]{:S(2)}) collective-permute-start(bf16[64,2048]{1,0:T(8,128)(2,1)S(1)} %combine.6), channel_id=1, source_target_pairs={{0,8},{8,16},{16,24},{1,9},{9,17},{17,25},{2,10},{10,18},{18,26},{... | collective-permute-start | bytes 786440 | tf_op jit(solution)/shard_map/ppermute | solution.py:281
  151.2 8.3 %collective-permute-start.4 = (bf16[64,2048]{1,0:T(8,128)(2,1)S(1)}, bf16[64,2048]{1,0:T(8,128)(2,1)S(1)}, u32[]{:S(2)}, u32[]{:S(2)}) collective-permute-start(bf16[64,2048]{1,0:T(8,128)(2,1)S(1)} %combine.7), channel_id=1, source_target_pairs={{0,8},{8,16},{16,24},{1,9},{9,17},{17,25},{2,10},{10,18},{18,26},{... | collective-permute-start | bytes 786440 | tf_op jit(solution)/shard_map/ppermute | solution.py:281
  166.3 10.8 %all-to-all-start.7 = ((bf16[4,40,2048]{2,1,0:T(8,128)(2,1)}), bf16[4,40,2048]{2,1,0:T(8,128)(2,1)S(1)}, u32[]{:S(2)}, u32[]{:S(2)}) async-start(bf16[4,40,2048]{2,1,0:T(8,128)(2,1)} %bitcast.28), calls=%async_computation.7 | async-start | bytes 1310720 | tf_op jit(solution)/shard_map/all_to_all | solution.py:255
  189.4 10.8 %all-to-all-start.8 = ((bf16[4,40,2048]{2,1,0:T(8,128)(2,1)}), bf16[4,40,2048]{2,1,0:T(8,128)(2,1)S(1)}, u32[]{:S(2)}, u32[]{:S(2)}) async-start(bf16[4,40,2048]{2,1,0:T(8,128)(2,1)} %bitcast.30), calls=%async_computation.8 | async-start | bytes 1310720 | tf_op jit(solution)/shard_map/all_to_all | solution.py:255
  200.6 8.3 %collective-permute-start.5 = (bf16[64,2048]{1,0:T(8,128)(2,1)S(1)}, bf16[64,2048]{1,0:T(8,128)(2,1)S(1)}, u32[]{:S(2)}, u32[]{:S(2)}) collective-permute-start(bf16[64,2048]{1,0:T(8,128)(2,1)S(1)} %combine.8), channel_id=1, source_target_pairs={{0,8},{8,16},{16,24},{1,9},{9,17},{17,25},{2,10},{10,18},{18,26},{... | collective-permute-start | bytes 786440 | tf_op jit(solution)/shard_map/ppermute | solution.py:281
  215.7 10.8 %all-to-all-start.9 = ((bf16[4,40,2048]{2,1,0:T(8,128)(2,1)}), bf16[4,40,2048]{2,1,0:T(8,128)(2,1)S(1)}, u32[]{:S(2)}, u32[]{:S(2)}) async-start(bf16[4,40,2048]{2,1,0:T(8,128)(2,1)} %bitcast.34), calls=%async_computation.9 | async-start | bytes 1310720 | tf_op jit(solution)/shard_map/all_to_all | solution.py:255
  238.8 10.8 %all-to-all-start.10 = ((bf16[4,40,2048]{2,1,0:T(8,128)(2,1)}), bf16[4,40,2048]{2,1,0:T(8,128)(2,1)S(1)}, u32[]{:S(2)}, u32[]{:S(2)}) async-start(bf16[4,40,2048]{2,1,0:T(8,128)(2,1)} %bitcast.36), calls=%async_computation.10 | async-start | bytes 1310720 | tf_op jit(solution)/shard_map/all_to_all | solution.py:255
  250.0 0.8 copy-start.1

commit v3 on v2

v3 whole, which is shorter than its diff:
```python
import functools
import math

import jax
import jax.numpy as jnp
from jax import lax
from jax.experimental import pallas as pl
from jax.experimental.pallas import tpu as pltpu
from jax.sharding import PartitionSpec as P

HEAD_DIM = 128
CAND_LEN = 64
CAND_DEV = 2
HIDDEN_CHUNK = 512
MIB = 1 << 20

EPSILON = 1e-05

VMEM = pl.BlockSpec(memory_space=pltpu.VMEM)
SMEM = pl.BlockSpec(memory_space=pltpu.SMEM)
HBM = pl.BlockSpec(memory_space=pltpu.HBM)
F32 = jnp.float32
BF16 = jnp.bfloat16


def in_hbm(*arrays):
    return [pltpu.with_memory_space_constraint(array, pltpu.HBM) for array in arrays]


def in_vmem(*arrays):
    return [pltpu.with_memory_space_constraint(array, pltpu.VMEM) for array in arrays]


def normalize(carried, gain_row):
    average = jnp.mean(carried, axis=-1, keepdims=True)
    centered = carried - average
    variance = jnp.mean(centered * centered, axis=-1, keepdims=True)
    return gain_row * centered * lax.rsqrt(variance + EPSILON)


def dot(left, right, contract=((1,), (0,))):
    return lax.dot_general(left, right, (contract, ((), ())), preferred_element_type=F32)


def attend_kernel(step, capacity, scalars, *refs):
    incoming = states = None
    if step > 0:
        incoming, refs = refs[0], refs[1:]
    if step < CAND_DEV:
        states, refs = refs[0], refs[1:]
    stream = step == 0
    (routes, cached, attn_gain, ffn_gain, router_t, w_query, w_out,
     after_ref, outgoing, weights), refs = refs[:10], refs[10:]
    if stream:
        sources, (w_query, w_out), refs = (w_query, w_out), refs[:2], refs[2:]
    fresh, gain_buf, router_buf, context, sems = refs
    segment = scalars[0]
    fills = [
        (attn_gain, gain_buf.at[0]),
        (ffn_gain, gain_buf.at[1]),
        (router_t, router_buf),
    ]
    if stream:
        fills += [(sources[0], w_query), (sources[1], w_out)]
    if states is not None:
        fills.insert(0, (states.at[pl.ds(step * CAND_LEN, CAND_LEN), :], fresh))
    copies = [pltpu.make_async_copy(*pair, sems.at[i]) for i, pair in enumerate(fills)]
    for copy in copies:
        copy.start()
    if states is not None:
        copies[0].wait()
        copies = copies[1:]

    if step == 0:
        current = fresh[...]
    elif step < CAND_DEV:
        current = jnp.where(segment == 0, fresh[...], incoming[...])
    else:
        current = incoming[...]
    copies[0].wait()
    copies[1].wait()
    carried = current.astype(F32)
    normed = normalize(carried, gain_buf[0]).astype(BF16)
    if stream:
        copies[3].wait()
    queries = dot(normed, w_query[...]).astype(BF16)
    head_total = queries.shape[1]
    scale = 1.0 / math.sqrt(HEAD_DIM)
    for start in range(0, head_total, HEAD_DIM):
        lanes = slice(start, start + HEAD_DIM)
        scores = dot(queries[:, lanes], cached[:, lanes], ((1,), (1,))) * scale
        exponent = jnp.exp(scores - jnp.max(scores, axis=1, keepdims=True))
        share = (exponent / jnp.sum(exponent, axis=1, keepdims=True)).astype(BF16)
        values = cached[:, head_total + start : head_total + start + HEAD_DIM]
        context[:, lanes] = dot(share, values).astype(BF16)
    if stream:
        copies[4].wait()
    after_attn = carried + dot(context[...], w_out[...])
    after_ref[...] = after_attn
    ffn_input = normalize(after_attn, gain_buf[1]).astype(BF16)

    rows, experts = after_attn.shape[0], router_t.shape[0]
    copies[2].wait()
    logits = dot(ffn_input, router_buf[...], ((1,), (1,)))
    micro = jnp.clip(step - segment, 0, CAND_DEV - 1)
    live = lax.broadcasted_iota(jnp.int32, (rows, 1), 0) < scalars[1 + micro]
    route = routes[micro]
    labels = lax.broadcasted_iota(jnp.int32, (rows, experts), 1)
    first, second = route[:, 0:1] == labels, route[:, 1:2] == labels
    logit_first = jnp.sum(jnp.where(first, logits, 0.0), axis=1, keepdims=True)
    logit_second = jnp.sum(jnp.where(second, logits, 0.0), axis=1, keepdims=True)
    gate_first = jax.nn.sigmoid(logit_first - logit_second)
    gate_second = 1.0 - gate_first
    named = jnp.where((first | second) & live, 1.0, 0.0).astype(BF16)
    earlier = lax.broadcasted_iota(jnp.int32, (rows, rows), 1) < lax.broadcasted_iota(
        jnp.int32, (rows, rows), 0
    )
    before = dot(jnp.where(earlier, 1.0, 0.0).astype(BF16), named)
    slots = lax.broadcasted_iota(jnp.int32, (rows, experts * capacity), 1)
    chosen = []
    for mask, column in ((first, 0), (second, 1)):
        slot = jnp.sum(jnp.where(mask, before, 0.0), axis=1, keepdims=True).astype(jnp.int32)
        target = route[:, column : column + 1] * capacity + slot
        chosen.append((slots == target) & live)
    select = jnp.where(chosen[0] | chosen[1], 1.0, 0.0).astype(BF16)
    outgoing[...] = dot(select, ffn_input, ((0,), (0,))).astype(BF16)
    weights[...] = jnp.where(chosen[0], gate_first, 0.0) + jnp.where(chosen[1], gate_second, 0.0)


def attend(step, capacity, scalars, states, incoming, routes, cached, gains, router_t, mats):
    w_query, w_out = mats
    width, head_total = w_query.shape
    slot_count = router_t.shape[0] * capacity
    stream = step == 0
    sources, specs = [], []
    if step > 0:
        sources.append(incoming)
        specs.append(VMEM)
    if step < CAND_DEV:
        sources += in_hbm(states)
        specs.append(HBM)
    out_shape = [
        jax.ShapeDtypeStruct((CAND_LEN, width), F32),
        jax.ShapeDtypeStruct((slot_count, width), BF16),
        jax.ShapeDtypeStruct((CAND_LEN, slot_count), F32),
    ]
    if stream:
        out_shape += [pltpu.VMEM(mat.shape, BF16) for mat in mats]
    outs = pl.pallas_call(
        functools.partial(attend_kernel, step, capacity),
        in_specs=[SMEM] + specs + [VMEM, VMEM, HBM, HBM, HBM] + [HBM if stream else VMEM] * 2,
        out_specs=[VMEM] * len(out_shape),
        out_shape=out_shape,
        scratch_shapes=[
            pltpu.VMEM((CAND_LEN, width), BF16),
            pltpu.VMEM((2, 1, width), F32),
            pltpu.VMEM(router_t.shape, BF16),
            pltpu.VMEM((CAND_LEN, head_total), BF16),
            pltpu.SemaphoreType.DMA((6,)),
        ],
        compiler_params=pltpu.CompilerParams(vmem_limit_bytes=12 * MIB),
        cost_estimate=pl.CostEstimate(
            flops=6 * CAND_LEN * width * head_total,
            bytes_accessed=4 * width * head_total + 8 * CAND_LEN * width,
            transcendentals=0,
        ),
        name="attend",
    )(
        scalars, *sources, routes, cached, *in_hbm(*gains, router_t),
        *(in_hbm(*mats) if stream else in_vmem(*mats)),
    )
    return outs[:3], (outs[3:] if stream else mats)


def expert_kernel(stream, rows, *refs):
    size = HIDDEN_CHUNK
    if stream:
        sources, served, mats, refs = refs[:4], refs[4], refs[5:9], refs[9:]
        own_hidden, other_hidden, sems = refs
    else:
        mats, (served, own_hidden, other_hidden) = refs[:4], refs[4:]
    own_in, own_down, other_in, other_down = mats

    def chunk_of(i):
        return pl.ds(pl.multiple_of(i * size, size), size)

    def fill(mat, i):
        lanes = chunk_of(i)
        return pltpu.make_async_copy(
            sources[mat].at[:, lanes], mats[mat].at[:, lanes], sems.at[mat, i]
        )

    if stream:
        for pair in ((0, 2), (1, 3)):
            for i in range(own_in.shape[1] // size):
                for mat in pair:
                    fill(mat, i).start()

    @pl.loop(0, own_in.shape[1] // size)
    def _(i):
        units = chunk_of(i)
        if stream:
            fill(0, i).wait()
        own_hidden[:, units] = jnp.maximum(dot(rows[...], own_in[:, units]), 0.0).astype(BF16)
        if stream:
            fill(2, i).wait()
        other_hidden[:, units] = jnp.maximum(dot(rows[...], other_in[:, units]), 0.0).astype(BF16)

    @pl.loop(0, own_down.shape[1] // size)
    def _(i):
        lanes = chunk_of(i)
        if stream:
            fill(1, i).wait()
            fill(3, i).wait()
        served[:, lanes] = (
            dot(own_hidden[...], own_down[:, lanes]) + dot(other_hidden[...], other_down[:, lanes])
        ).astype(BF16)


def expert_rows(rows, mats, stream):
    count, width = rows.shape
    units = mats[0].shape[1]
    scratch = [pltpu.VMEM((count, units), BF16), pltpu.VMEM((count, units), BF16)]
    out_shape = [jax.ShapeDtypeStruct(rows.shape, BF16)]
    if stream:
        scratch.append(pltpu.SemaphoreType.DMA((4, units // HIDDEN_CHUNK)))
        out_shape += [pltpu.VMEM(mat.shape, BF16) for mat in mats]
    outs = pl.pallas_call(
        functools.partial(expert_kernel, stream),
        in_specs=[VMEM] + [HBM if stream else VMEM] * 4,
        out_specs=[VMEM] * len(out_shape),
        out_shape=out_shape,
        scratch_shapes=scratch,
        compiler_params=pltpu.CompilerParams(vmem_limit_bytes=12 * MIB),
        cost_estimate=pl.CostEstimate(
            flops=8 * count * width * units,
            bytes_accessed=8 * width * units + 4 * count * width,
            transcendentals=0,
        ),
        name="experts",
    )(rows, *(in_hbm(*mats) if stream else in_vmem(*mats)))
    return outs[0], (outs[1:] if stream else mats)


def mixed(after_attn, weights, expert_out):
    gates = weights[...]
    coarse = gates.astype(BF16)
    fine = (gates - coarse.astype(F32)).astype(BF16)
    rows = expert_out[...]
    return (after_attn[...] + (dot(coarse, rows) + dot(fine, rows))).astype(BF16)


def combine_kernel(after_attn, weights, expert_out, result):
    result[...] = mixed(after_attn, weights, expert_out)


def place_kernel(after_attn, weights, expert_out, scalars, *refs):
    earlier, (output, result, sems) = refs[:-3], refs[-3:]
    segment = scalars[0]

    def place(source, micro):
        rows = pl.ds(micro * CAND_LEN, CAND_LEN)
        return pltpu.make_async_copy(source, output.at[rows, :], sems.at[micro])

    last = len(earlier)
    for micro in range(CAND_DEV):
        for step in range(micro, last):

            @pl.when(segment + micro == step)
            def _():
                place(earlier[step], micro).start()

    result[...] = mixed(after_attn, weights, expert_out)
    for micro in range(CAND_DEV):

        @pl.when(segment + micro == last)
        def _():
            place(result, micro).start()

    for micro in range(CAND_DEV):
        place(result, micro).wait()


def combine(after_attn, weights, expert_out, scalars=None, earlier=()):
    rows, width = after_attn.shape
    inputs = [after_attn, weights, expert_out]
    specs = [VMEM] * 3
    scratch = []
    out_shape, out_spec = jax.ShapeDtypeStruct((rows, width), BF16), VMEM
    if earlier:
        inputs += [scalars, *in_hbm(*earlier)]
        specs += [SMEM] + [HBM] * len(earlier)
        scratch = [pltpu.VMEM((rows, width), BF16), pltpu.SemaphoreType.DMA((CAND_DEV,))]
        out_shape, out_spec = jax.ShapeDtypeStruct((CAND_DEV * rows, width), BF16), HBM
    return pl.pallas_call(
        place_kernel if earlier else combine_kernel,
        in_specs=specs,
        out_specs=out_spec,
        out_shape=out_shape,
        scratch_shapes=scratch,
        compiler_params=pltpu.CompilerParams(vmem_limit_bytes=8 * MIB),
        cost_estimate=pl.CostEstimate(
            flops=4 * weights.size * width,
            bytes_accessed=6 * after_attn.size + 2 * expert_out.size,
            transcendentals=0,
        ),
        name="combine",
    )(*inputs)


def local(
    states, cand_len, routes, enc_kv, attn_gain, ffn_gain, w_query, w_out, w_router, w_in, w_down
):
    segment_index = lax.axis_index("segment")
    n_segment = lax.axis_size("segment")
    n_expert = lax.axis_size("expert")
    model_width = states.shape[1]
    experts = w_router.shape[2]
    capacity = 2 * ((5 * CAND_LEN + 4 * experts - 1) // (4 * experts))
    core_pairs = [(i, i ^ 1) for i in range(n_expert)]
    same_core = [list(range(core, n_expert, 2)) for core in range(2)]

    def exchange(rows):
        blocks = rows.reshape(experts, capacity, model_width)
        moved = lax.all_to_all(
            blocks, "expert", split_axis=0, concat_axis=0, axis_index_groups=same_core, tiled=True
        )
        return moved.reshape(rows.shape)

    spread = jnp.repeat(enc_kv[:, 0, :], n_expert, axis=0)
    cached = lax.all_to_all(
        spread, ("segment", "expert"), split_axis=0, concat_axis=0, tiled=True
    )
    own = (w_in[0, 0], w_down[0, 0])
    other = tuple(lax.ppermute(mat, "expert", core_pairs) for mat in own)

    scalars = jnp.concatenate([segment_index.astype(jnp.int32).reshape(1), cand_len])
    route_all = routes[0].reshape(CAND_DEV, CAND_LEN, 2)
    router_t = w_router[0].T
    attend_mats = (w_query[0], w_out[0])
    expert_mats = (*own, *other)
    step_count = CAND_DEV + n_segment - 1
    incoming = None
    earlier = []
    for step in range(step_count):
        (after_attn, outgoing, weights), attend_mats = attend(
            step, capacity, scalars, states, incoming, route_all, cached,
            (attn_gain, ffn_gain), router_t, attend_mats,
        )
        served, expert_mats = expert_rows(exchange(outgoing), expert_mats, step == 0)
        expert_out = exchange(served)
        if step + 1 < step_count:
            result = combine(after_attn, weights, expert_out)
            incoming = lax.ppermute(
                result, "segment", [(i, i + 1) for i in range(n_segment - 1)]
            )
            earlier.append(result)
    output = combine(after_attn, weights, expert_out, scalars, earlier)
    return output.reshape(1, CAND_DEV * CAND_LEN, model_width)


def solution(mesh):
    return jax.shard_map(
        local,
        mesh=mesh,
        in_specs=(
            P("expert", None),
            P("expert"),
            P("segment", "expert", None),
            P(None, ("segment", "expert"), None),
            P("segment", None),
            P("segment", None),
            P("segment", None, None),
            P("segment", None, None),
            P("segment", None, None),
            P("segment", "expert", None, None),
            P("segment", "expert", None, None),
        ),
        out_specs=P("segment", "expert", None),
        check_vma=False,
    )
```

time: 252 us -> 243 us (0.964)
  blocking collectives: 65.8 us -> 107 us
  waiting for transfers between devices: 50.8 us -> 22.1 us
  starting transfers between devices: 36.3 us -> 22.3 us
  Pallas kernels: 92.5 us -> 83.4 us
    all_to_all x6 -> x10, blocking collectives: 65.8 us -> 107 us  [exchange(): lax.all_to_all(blocks, 'expert', split_axis=0, concat_axis=0, axis_index_...]
    all_to_all x4 -> x0, waiting for transfers between devices: 28.8 us -> none  [exchange(): lax.all_to_all(blocks, 'expert', split_axis=0, concat_axis=0, axis_index_...]
    all_to_all x4 -> x0, starting transfers between devices: 14 us -> none  [exchange(): lax.all_to_all(blocks, 'expert', split_axis=0, concat_axis=0, axis_index_...]
    pallas_call x5, Pallas kernels: 31.7 us -> 24.5 us  [attend(): pl.pallas_call(functools.partial(attend_kernel, step, capacity), in_specs...]
    unnamed x8 -> x20, local copies, waits for them, and re-layouts: 2.68 us -> 5.3 us
  transfers between devices with their start and end apart: 11 -> 7, of which waited for: 9 -> 5; matrix products, arithmetic and copies ran while one was open for 2% -> 2% of each run, Pallas kernels for 2% -> 3%
where the time goes in v3:
time: 243 us; the launch traced here: 242 us
  blocking collectives  107 us (44%)
  Pallas kernels  83.4 us (34%)
  starting transfers between devices  22.3 us (9%)
  waiting for transfers between devices  22.1 us (9%)
  local copies, waits for them, and re-layouts  5.83 us (2%)
    all_to_all x10, blocking collectives, exchange(): lax.all_to_all(blocks, 'expert', split_axis=0, concat_axis=0, axis_index_...  107 us
    pallas_call x5, Pallas kernels, expert_rows(): pl.pallas_call(functools.partial(expert_kernel, stream), in_specs=[VMEM]...  40.1 us
    pallas_call x5, Pallas kernels, attend(): pl.pallas_call(functools.partial(attend_kernel, step, capacity), in_specs...  24.5 us
    pallas_call x5, Pallas kernels, combine(): pl.pallas_call(place_kernel if earlier else combine_kernel, in_specs=spec...  18.9 us
    ppermute x4, waiting for transfers between devices, local(): lax.ppermute(result, 'segment', [(i, i + 1) for i in range(n_segment - 1)])  15.4 us
    ppermute x4, starting transfers between devices, local(): lax.ppermute(result, 'segment', [(i, i + 1) for i in range(n_segment - 1)])  14.5 us
    all_to_all x1, starting transfers between devices, local(): lax.all_to_all(spread, ('segment', 'expert'), split_axis=0, concat_axis=0...  7.3 us
    all_to_all x1, waiting for transfers between devices, local(): lax.all_to_all(spread, ('segment', 'expert'), split_axis=0, concat_axis=0...  6.71 us
  transfers between devices with their start and end apart: 7, of which 5 were waited for; matrix products, arithmetic and copies ran while one was open for 2% of the time, Pallas kernels for 3%

profile of v3, /device:TPU:0, one launch (start us, length us, event | category | flops | bytes accessed | tf_op | source)
XLA Modules:
  0.0 242.2 jit_solution(10207928297680052753)
XLA Ops:
  2.7 7.3 %all-to-all-start = ((bf16[32,2,1024]{2,1,0:T(2,128)(2,1)}), bf16[32,2,1024]{2,1,0:T(2,128)(2,1)S(1)}, u32[]{:S(2)}, u32[]{:S(2)}) async-start(bf16[32,2,1024]{2,1,0:T(2,128)(2,1)} %reshape.92), calls=%async_computation | async-start | bytes 262144 | tf_op jit(solution)/shard_map/all_to_all | solution.py:331
  11.5 6.7 %all-to-all-done = bf16[32,2,1024]{2,1,0:T(2,128)(2,1)S(1)} async-done(((bf16[32,2,1024]{2,1,0:T(2,128)(2,1)}), bf16[32,2,1024]{2,1,0:T(2,128)(2,1)S(1)}, u32[]{:S(2)}, u32[]{:S(2)}) %all-to-all-start) | async-done | bytes 131104 | tf_op jit(solution)/shard_map/all_to_all | solution.py:331
  18.4 6.1 %attend.5 = (f32[64,2048]{1,0:T(8,128)S(1)}, bf16[160,2048]{1,0:T(8,128)(2,1)S(1)}, f32[64,160]{1,0:T(8,128)S(1)}, bf16[2048,1024]{1,0:T(8,128)(2,1)S(1)}, bf16[1024,2048]{1,0:T(8,128)(2,1)S(1)}) custom-call(s32[3]{0:T(128)S(1)} %pad_add_fusion.scalars, bf16[128,2048]{1,0:T(8,128)(2,1)} %refs_1_.1, s32[2,64,2]{2,1,0:T(8,128)S(1)} %bitcast.56, ...), custom_call_target="tpu_custom_call" | custom-call | flops 805306368 | bytes 9437184 | tf_op jit(solution)/shard_map/attend/pallas_call | solution.py:149
  24.5 13.0 %all_to_all.61 = bf16[4,40,2048]{2,1,0:T(8,128)(2,1)S(1)} all-to-all(bf16[4,40,2048]{2,1,0:T(8,128)(2,1)S(1)} %bitcast.63), channel_id=1, replica_groups={{0,2,4,6},{1,3,5,7},{8,10,12,14},{9,11,13,15},{16,18,20,22},{17,19,21,2..., dimensions={0} | all-to-all | bytes 1310720 | tf_op jit(solution)/shard_map/all_to_all | solution.py:325
  37.5 11.9 %experts.5 = (bf16[160,2048]{1,0:T(8,128)(2,1)S(1)}, bf16[2048,2048]{1,0:T(8,128)(2,1)S(1)}, bf16[2048,2048]{1,0:T(8,128)(2,1)S(1)}, bf16[2048,2048]{1,0:T(8,128)(2,1)S(1)}, bf16[2048,2048]{1,0:T(8,128)(2,1)S(1)}) custom-call(bf16[160,2048]{1,0:T(8,128)(2,1)S(1)} %bitcast.47, bf16[2048,2048]{1,0:T(8,128)(2,1)} %bitcast.68, bf16[2048,2048]{1,0:T(8,128)(2,1)} %bitcast.70, ...), custom_call_target="tpu_custom_call" | custom-call | flops 5368709120 | bytes 34865152 | tf_op jit(solution)/shard_map/experts/pallas_call | solution.py:228
  49.4 11.8 %all_to_all.62 = bf16[4,40,2048]{2,1,0:T(8,128)(2,1)S(1)} all-to-all(bf16[4,40,2048]{2,1,0:T(8,128)(2,1)S(1)} %bitcast.61), channel_id=1, replica_groups={{0,2,4,6},{1,3,5,7},{8,10,12,14},{9,11,13,15},{16,18,20,22},{17,19,21,2..., dimensions={0} | all-to-all | bytes 1310720 | tf_op jit(solution)/shard_map/all_to_all | solution.py:325
  61.6 1.3 collective-permute-start.2
  62.9 3.9 %collective-permute-done.2.refs_0_ = bf16[64,2048]{1,0:T(8,128)(2,1)S(1)} collective-permute-done((bf16[64,2048]{1,0:T(8,128)(2,1)S(1)}, bf16[64,2048]{1,0:T(8,128)(2,1)S(1)}, u32[]{:S(2)}, u32[]{:S(2)}) %collective-permute-start.2) | collective-permute-done | bytes 262176 | tf_op jit(solution)/shard_map/ppermute | solution.py:354
  66.8 4.8 %attend.6 = (f32[64,2048]{1,0:T(8,128)S(1)}, bf16[160,2048]{1,0:T(8,128)(2,1)S(1)}, f32[64,160]{1,0:T(8,128)S(1)}) custom-call(s32[3]{0:T(128)S(1)} %pad_add_fusion.scalars, bf16[64,2048]{1,0:T(8,128)(2,1)S(1)} %collective-permute-done.2.refs_0_, bf16[128,2048]{1,0:T(8,128)(2,1)} %refs_1_.1, s32[2,64,2]{2,1,0:T(8,128)S(1)} %bitcast.57, ...), custom_call_target="tpu_custom_call" | custom-call | flops 805306368 | bytes 9437184 | tf_op jit(solution)/shard_map/attend/pallas_call | solution.py:149
  71.6 10.2 %all_to_all.63 = bf16[4,40,2048]{2,1,0:T(8,128)(2,1)S(1)} all-to-all(bf16[4,40,2048]{2,1,0:T(8,128)(2,1)S(1)} %bitcast.64), channel_id=1, replica_groups={{0,2,4,6},{1,3,5,7},{8,10,12,14},{9,11,13,15},{16,18,20,22},{17,19,21,2..., dimensions={0} | all-to-all | bytes 1310720 | tf_op jit(solution)/shard_map/all_to_all | solution.py:325
  81.8 7.1 %experts.6 = bf16[160,2048]{1,0:T(8,128)(2,1)S(1)} custom-call(bf16[160,2048]{1,0:T(8,128)(2,1)S(1)} %bitcast.50, bf16[2048,2048]{1,0:T(8,128)(2,1)S(1)} %get-tuple-element.36.refs_0_, bf16[2048,2048]{1,0:T(8,128)(2,1)S(1)} %get-tuple-element.37.refs_1_, bf16[2048,2048]{1,0:T(8,128)(2,1)S(1)} %get-tuple-element.38.refs_2_, ...), custom_call_target="tpu_custom_call" | custom-call | flops 5368709120 | bytes 34865152 | tf_op jit(solution)/shard_map/experts/pallas_call | solution.py:228
  88.9 10.2 %all_to_all.64 = bf16[4,40,2048]{2,1,0:T(8,128)(2,1)S(1)} all-to-all(bf16[4,40,2048]{2,1,0:T(8,128)(2,1)S(1)} %bitcast.51), channel_id=1, replica_groups={{0,2,4,6},{1,3,5,7},{8,10,12,14},{9,11,13,15},{16,18,20,22},{17,19,21,2..., dimensions={0} | all-to-all | bytes 1310720 | tf_op jit(solution)/shard_map/all_to_all | solution.py:325
  99.5 4.4 %collective-permute-start.3 = (bf16[64,2048]{1,0:T(8,128)(2,1)S(1)}, bf16[64,2048]{1,0:T(8,128)(2,1)S(1)}, u32[]{:S(2)}, u32[]{:S(2)}) collective-permute-start(bf16[64,2048]{1,0:T(8,128)(2,1)S(1)} %combine.6.refs_1_), channel_id=1, source_target_pairs={{0,8},{8,16},{16,24},{1,9},{9,17},{17,25},{2,10},{10,18},{18,26},{... | collective-permute-start | bytes 786440 | tf_op jit(solution)/shard_map/ppermute | solution.py:354
  103.9 3.9 %collective-permute-done.3.refs_0_ = bf16[64,2048]{1,0:T(8,128)(2,1)S(1)} collective-permute-done((bf16[64,2048]{1,0:T(8,128)(2,1)S(1)}, bf16[64,2048]{1,0:T(8,128)(2,1)S(1)}, u32[]{:S(2)}, u32[]{:S(2)}) %collective-permute-start.3) | collective-permute-done | bytes 262176 | tf_op jit(solution)/shard_map/ppermute | solution.py:354
  107.8 4.5 %attend.7 = (f32[64,2048]{1,0:T(8,128)S(1)}, bf16[160,2048]{1,0:T(8,128)(2,1)S(1)}, f32[64,160]{1,0:T(8,128)S(1)}) custom-call(s32[3]{0:T(128)S(1)} %pad_add_fusion.scalars, bf16[64,2048]{1,0:T(8,128)(2,1)S(1)} %collective-permute-done.3.refs_0_, s32[2,64,2]{2,1,0:T(8,128)S(1)} %bitcast.58, bf16[32,2048]{1,0:T(8,128)(2,1)S(1)} %bitcast.39, ...), custom_call_target="tpu_custom_call" | custom-call | flops 805306368 | bytes 9437184 | tf_op jit(solution)/shard_map/attend/pallas_call | solution.py:149
  112.3 10.2 %all_to_all.65 = bf16[4,40,2048]{2,1,0:T(8,128)(2,1)S(1)} all-to-all(bf16[4,40,2048]{2,1,0:T(8,128)(2,1)S(1)} %bitcast.65), channel_id=1, replica_groups={{0,2,4,6},{1,3,5,7},{8,10,12,14},{9,11,13,15},{16,18,20,22},{17,19,21,2..., dimensions={0} | all-to-all | bytes 1310720 | tf_op jit(solution)/shard_map/all_to_all | solution.py:325
  122.5 7.0 %experts.7 = bf16[160,2048]{1,0:T(8,128)(2,1)S(1)} custom-call(bf16[160,2048]{1,0:T(8,128)(2,1)S(1)} %bitcast.52, bf16[2048,2048]{1,0:T(8,128)(2,1)S(1)} %get-tuple-element.36.refs_0_, bf16[2048,2048]{1,0:T(8,128)(2,1)S(1)} %get-tuple-element.37.refs_1_, bf16[2048,2048]{1,0:T(8,128)(2,1)S(1)} %get-tuple-element.38.refs_2_, ...), custom_call_target="tpu_custom_call" | custom-call | flops 5368709120 | bytes 34865152 | tf_op jit(solution)/shard_map/experts/pallas_call | solution.py:228
  129.6 10.2 %all_to_all.66 = bf16[4,40,2048]{2,1,0:T(8,128)(2,1)S(1)} all-to-all(bf16[4,40,2048]{2,1,0:T(8,128)(2,1)S(1)} %bitcast.53), channel_id=1, replica_groups={{0,2,4,6},{1,3,5,7},{8,10,12,14},{9,11,13,15},{16,18,20,22},{17,19,21,2..., dimensions={0} | all-to-all | bytes 1310720 | tf_op jit(solution)/shard_map/all_to_all | solution.py:325
  140.2 4.4 %collective-permute-start.4 = (bf16[64,2048]{1,0:T(8,128)(2,1)S(1)}, bf16[64,2048]{1,0:T(8,128)(2,1)S(1)}, u32[]{:S(2)}, u32[]{:S(2)}) collective-permute-start(bf16[64,2048]{1,0:T(8,128)(2,1)S(1)} %combine.7.refs_2_), channel_id=1, source_target_pairs={{0,8},{8,16},{16,24},{1,9},{9,17},{17,25},{2,10},{10,18},{18,26},{... | collective-permute-start | bytes 786440 | tf_op jit(solution)/shard_map/ppermute | solution.py:354
  144.6 3.9 %collective-permute-done.4.refs_0_ = bf16[64,2048]{1,0:T(8,128)(2,1)S(1)} collective-permute-done((bf16[64,2048]{1,0:T(8,128)(2,1)S(1)}, bf16[64,2048]{1,0:T(8,128)(2,1)S(1)}, u32[]{:S(2)}, u32[]{:S(2)}) %collective-permute-start.4) | collective-permute-done | bytes 262176 | tf_op jit(solution)/shard_map/ppermute | solution.py:354
  148.4 4.5 %attend.8 = (f32[64,2048]{1,0:T(8,128)S(1)}, bf16[160,2048]{1,0:T(8,128)(2,1)S(1)}, f32[64,160]{1,0:T(8,128)S(1)}) custom-call(s32[3]{0:T(128)S(1)} %pad_add_fusion.scalars, bf16[64,2048]{1,0:T(8,128)(2,1)S(1)} %collective-permute-done.4.refs_0_, s32[2,64,2]{2,1,0:T(8,128)S(1)} %bitcast.59, bf16[32,2048]{1,0:T(8,128)(2,1)S(1)} %bitcast.40, ...), custom_call_target="tpu_custom_call" | custom-call | flops 805306368 | bytes 9437184 | tf_op jit(solution)/shard_map/attend/pallas_call | solution.py:149
  153.0 10.2 %all_to_all.67 = bf16[4,40,2048]{2,1,0:T(8,128)(2,1)S(1)} all-to-all(bf16[4,40,2048]{2,1,0:T(8,128)(2,1)S(1)} %bitcast.66), channel_id=1, replica_groups={{0,2,4,6},{1,3,5,7},{8,10,12,14},{9,11,13,15},{16,18,20,22},{17,19,21,2..., dimensions={0} | all-to-all | bytes 1310720 | tf_op jit(solution)/shard_map/all_to_all | solution.py:325
  163.2 7.0 %experts.8 = bf16[160,2048]{1,0:T(8,128)(2,1)S(1)} custom-call(bf16[160,2048]{1,0:T(8,128)(2,1)S(1)} %bitcast.54, bf16[2048,2048]{1,0:T(8,128)(2,1)S(1)} %get-tuple-element.36.refs_0_, bf16[2048,2048]{1,0:T(8,128)(2,1)S(1)} %get-tuple-element.37.refs_1_, bf16[2048,2048]{1,0:T(8,128)(2,1)S(1)} %get-tuple-element.38.refs_2_, ...), custom_call_target="tpu_custom_call" | custom-call | flops 5368709120 | bytes 34865152 | tf_op jit(solution)/shard_map/experts/pallas_call | solution.py:228
  170.3 10.2 %all_to_all.68 = bf16[4,40,2048]{2,1,0:T(8,128)(2,1)S(1)} all-to-all(bf16[4,40,2048]{2,1,0:T(8,128)(2,1)S(1)} %bitcast.55), channel_id=1, replica_groups={{0,2,4,6},{1,3,5,7},{8,10,12,14},{9,11,13,15},{16,18,20,22},{17,19,21,2..., dimensions={0} | all-to-all | bytes 1310720 | tf_op jit(solution)/shard_map/all_to_all | solution.py:325
  180.8 4.4 %collective-permute-start.5 = (bf16[64,2048]{1,0:T(8,128)(2,1)S(1)}, bf16[64,2048]{1,0:T(8,128)(2,1)S(1)}, u32[]{:S(2)}, u32[]{:S(2)}) collective-permute-start(bf16[64,2048]{1,0:T(8,128)(2,1)S(1)} %combine.8.refs_3_), channel_id=1, source_target_pairs={{0,8},{8,16},{16,24},{1,9},{9,17},{17,25},{2,10},{10,18},{18,26},{... | collective-permute-start | bytes 786440 | tf_op jit(solution)/shard_map/ppermute | solution.py:354
  185.2 3.9 %collective-permute-done.5.refs_0_ = bf16[64,2048]{1,0:T(8,128)(2,1)S(1)} collective-permute-done((bf16[64,2048]{1,0:T(8,128)(2,1)S(1)}, bf16[64,2048]{1,0:T(8,128)(2,1)S(1)}, u32[]{:S(2)}, u32[]{:S(2)}) %collective-permute-start.5) | collective-permute-done | bytes 262176 | tf_op jit(solution)/shard_map/ppermute | solution.py:354
  189.1 4.5 %attend.9 = (f32[64,2048]{1,0:T(8,128)S(1)}, bf16[160,2048]{1,0:T(8,128)(2,1)S(1)}, f32[64,160]{1,0:T(8,128)S(1)}) custom-call(s32[3]{0:T(128)S(1)} %pad_add_fusion.scalars, bf16[64,2048]{1,0:T(8,128)(2,1)S(1)} %collective-permute-done.5.refs_0_, s32[2,64,2]{2,1,0:T(8,128)S(1)} %bitcast.60, bf16[32,2048]{1,0:T(8,128)(2,1)S(1)} %bitcast.41, ...), custom_call_target="tpu_custom_call" | custom-call | flops 805306368 | bytes 9437184 | tf_op jit(solution)/shard_map/attend/pallas_call | solution.py:149
  193.6 10.2 %all_to_all.69 = bf16[4,40,2048]{2,1,0:T(8,128)(2,1)S(1)} all-to-all(bf16[4,40,2048]{2,1,0:T(8,128)(2,1)S(1)} %bitcast.62), channel_id=1, replica_groups={{0,2,4,6},{1,3,5,7},{8,10,12,14},{9,11,13,15},{16,18,20,22},{17,19,21,2..., dimensions={0} | all-to-all | bytes 1310720 | tf_op jit(solution)/shard_map/all_to_all | solution.py:325
  203.8 3.4 %copy-done.3 = bf16[2048,2048]{1,0:T(8,128)(2,1)S(1)} copy-done((bf16[2048,2048]{1,0:T(8,128)(2,1)S(1)}, bf16[2048,2048]{1,0:T(8,128)(2,1)}, u32[]{:S(2)}) %copy-start.3) | copy-done | bytes 8388632
  207.2 7.0 %experts.9 = bf16[160,2048]{1,0:T(8,128)(2,1)S(1)} custom-call(bf16[160,2048]{1,0:T(8,128)(2,1)S(1)} %bitcast.48, bf16[2048,2048]{1,0:T(8,128)(2,1)S(1)} %get-tuple-element.36.refs_0_, bf16[2048,2048]{1,0:T(8,128)(2,1)S(1)} %copy-done.3, bf16[2048,2048]{1,0:T(8,128)(2,1)S(1)} %get-tuple-element.38.refs_2_, bf16[2048,2048]{1,0:T(8,128)(2,1)S(1)} %get-tuple-element.39.refs_3_), custom_call_target="tpu_custom_call" | custom-call | flops 5368709120 | bytes 34865152 | tf_op jit(solution)/shard_map/experts/pallas_call | solution.py:228
  214.3 10.2 %all_to_all.70 = bf16[4,40,2048]{2,1,0:T(8,128)(2,1)S(1)} all-to-all(bf16[4,40,2048]{2,1,0:T(8,128)(2,1)S(1)} %bitcast.49), channel_id=1, replica_groups={{0,2,4,6},{1,3,5,7},{8,10,12,14},{9,11,13,15},{16,18,20,22},{17,19,21,2..., dimensions={0} | all-to-all | bytes 1310720 | tf_op jit(solution)/shard_map/all_to_all | solution.py:325
  224.5 17.5 %combine.9 = bf16[128,2048]{1,0:T(8,128)(2,1)} custom-call(f32[64,2048]{1,0:T(8,128)S(1)} %get-tuple-element.46.after_attn, f32[64,160]{1,0:T(8,128)S(1)} %get-tuple-element.47.weights, bf16[160,2048]{1,0:T(8,128)(2,1)S(1)} %bitcast.46, s32[3]{0:T(128)S(1)} %pad_add_fusion.scalars, bf16[64,2048]{1,0:T(8,128)(2,1)} %copy-done.4, bf16[64,2048]{1,0:T(8,128)(2,1)} %copy-done.5, ...), custom_call_target="tpu_custom_call" | custom-call | flops 83886080 | bytes 1441792 | tf_op jit(solution)/shard_map/combine/pallas_call | solution.py:295
  (31 shorter events, 5.8 us)
Async XLA Ops:
  0.0 0.7 copy-start
  0.0 37.5 %collective-permute-start = (bf16[2048,2048]{1,0:T(8,128)(2,1)}, bf16[2048,2048]{1,0:T(8,128)(2,1)}, u32[]{:S(2)}, u32[]{:S(2)}) collective-permute-start(bf16[2048,2048]{1,0:T(8,128)(2,1)} %bitcast.67), channel_id=1, source_target_pairs={{0,1},{1,0},{2,3},{3,2},{4,5},{5,4},{6,7},{7,6},{8,9},{9,8},{10,11... | collective-permute-start | bytes 25165832 | tf_op jit(solution)/shard_map/ppermute | solution.py:335
  0.5 37.1 %collective-permute-start.1 = (bf16[2048,2048]{1,0:T(8,128)(2,1)}, bf16[2048,2048]{1,0:T(8,128)(2,1)}, u32[]{:S(2)}, u32[]{:S(2)}) collective-permute-start(bf16[2048,2048]{1,0:T(8,128)(2,1)} %bitcast.69), channel_id=1, source_target_pairs={{0,1},{1,0},{2,3},{3,2},{4,5},{5,4},{6,7},{7,6},{8,9},{9,8},{10,11... | collective-permute-start | bytes 25165832 | tf_op jit(solution)/shard_map/ppermute | solution.py:335
  2.7 15.5 %all-to-all-start = ((bf16[32,2,1024]{2,1,0:T(2,128)(2,1)}), bf16[32,2,1024]{2,1,0:T(2,128)(2,1)S(1)}, u32[]{:S(2)}, u32[]{:S(2)}) async-start(bf16[32,2,1024]{2,1,0:T(2,128)(2,1)} %reshape.92), calls=%async_computation | async-start | bytes 262144 | tf_op jit(solution)/shard_map/all_to_all | solution.py:331
  49.4 113.8 %copy-start.2 = (bf16[2048,2048]{1,0:T(8,128)(2,1)}, bf16[2048,2048]{1,0:T(8,128)(2,1)S(1)}, u32[]{:S(2)}) copy-start(bf16[2048,2048]{1,0:T(8,128)(2,1)S(1)} %get-tuple-element.37.refs_1_) | copy-start | bytes 25165828
  61.6 27.3 %copy-start.4 = (bf16[64,2048]{1,0:T(8,128)(2,1)}, bf16[64,2048]{1,0:T(8,128)(2,1)S(1)}, u32[]{:S(2)}) copy-start(bf16[64,2048]{1,0:T(8,128)(2,1)S(1)} %combine.5.refs_0_) | copy-start | bytes 786436
  61.6 5.2 %collective-permute-start.2 = (bf16[64,2048]{1,0:T(8,128)(2,1)S(1)}, bf16[64,2048]{1,0:T(8,128)(2,1)S(1)}, u32[]{:S(2)}, u32[]{:S(2)}) collective-permute-start(bf16[64,2048]{1,0:T(8,128)(2,1)S(1)} %combine.5.refs_0_), channel_id=1, source_target_pairs={{0,8},{8,16},{16,24},{1,9},{9,17},{17,25},{2,10},{10,18},{18,26},{... | collective-permute-start | bytes 786440 | tf_op jit(solution)/shard_map/ppermute | solution.py:354
  99.5 30.0 %copy-start.5 = (bf16[64,2048]{1,0:T(8,128)(2,1)}, bf16[64,2048]{1,0:T(8,128)(2,1)S(1)}, u32[]{:S(2)}) copy-start(bf16[64,2048]{1,0:T(8,128)(2,1)S(1)} %combine.6.refs_1_) | copy-start | bytes 786436
  99.5 8.3 %collective-permute-start.3 = (bf16[64,2048]{1,0:T(8,128)(2,1)S(1)}, bf16[64,2048]{1,0:T(8,128)(2,1)S(1)}, u32[]{:S(2)}, u32[]{:S(2)}) collective-permute-start(bf16[64,2048]{1,0:T(8,128)(2,1)S(1)} %combine.6.refs_1_), channel_id=1, source_target_pairs={{0,8},{8,16},{16,24},{1,9},{9,17},{17,25},{2,10},{10,18},{18,26},{... | collective-permute-start | bytes 786440 | tf_op jit(solution)/shard_map/ppermute | solution.py:354
  140.1 30.1 %copy-start.6 = (bf16[64,2048]{1,0:T(8,128)(2,1)}, bf16[64,2048]{1,0:T(8,128)(2,1)S(1)}, u32[]{:S(2)}) copy-start(bf16[64,2048]{1,0:T(8,128)(2,1)S(1)} %combine.7.refs_2_) | copy-start | bytes 786436
  140.2 8.3 %collective-permute-start.4 = (bf16[64,2048]{1,0:T(8,128)(2,1)S(1)}, bf16[64,2048]{1,0:T(8,128)(2,1)S(1)}, u32[]{:S(2)}, u32[]{:S(2)}) collective-permute-start(bf16[64,2048]{1,0:T(8,128)(2,1)S(1)} %combine.7.refs_2_), channel_id=1, source_target_pairs={{0,8},{8,16},{16,24},{1,9},{9,17},{17,25},{2,10},{10,18},{18,26},{... | collective-permute-start | bytes 786440 | tf_op jit(solution)/shard_map/ppermute | solution.py:354
  180.8 33.4 %copy-start.7 = (bf16[64,2048]{1,0:T(8,128)(2,1)}, bf16[64,2048]{1,0:T(8,128)(2,1)S(1)}, u32[]{:S(2)}) copy-start(bf16[64,2048]{1,0:T(8,128)(2,1)S(1)} %combine.8.refs_3_) | copy-start | bytes 786436
  180.8 8.2 %collective-permute-start.5 = (bf16[64,2048]{1,0:T(8,128)(2,1)S(1)}, bf16[64,2048]{1,0:T(8,128)(2,1)S(1)}, u32[]{:S(2)}, u32[]{:S(2)}) collective-permute-start(bf16[64,2048]{1,0:T(8,128)(2,1)S(1)} %combine.8.refs_3_), channel_id=1, source_target_pairs={{0,8},{8,16},{16,24},{1,9},{9,17},{17,25},{2,10},{10,18},{18,26},{... | collective-permute-start | bytes 786440 | tf_op jit(solution)/shard_map/ppermute | solution.py:354
  203.8 3.4 %copy-start.3 = (bf16[2048,2048]{1,0:T(8,128)(2,1)S(1)}, bf16[2048,2048]{1,0:T(8,128)(2,1)}, u32[]{:S(2)}) copy-start(bf16[2048,2048]{1,0:T(8,128)(2,1)} %copy-done.2) | copy-start | bytes 25165828
  207.2 34.8 %copy-start.1 = (bf16[4,1,2048]{2,0,1:T(4,128)(2,1)S(1)}, bf16[4,1,2048]{2,0,1:T(4,128)(2,1)}, u32[]{:S(2)}) copy-start(bf16[4,1,2048]{2,0,1:T(4,128)(2,1)} %param.14) | copy-start | bytes 49156

commit v4 on v3

--- a/solution.py
+++ b/solution.py
@@ -42,26 +42,87 @@
     return lax.dot_general(left, right, (contract, ((), ())), preferred_element_type=F32)
 
 
+def spread_kernel(copies_of, enc_kv, blocks):
+    for layer in range(enc_kv.shape[0]):
+        block = enc_kv[layer]
+        for i in range(copies_of):
+            blocks[layer * copies_of + i] = block
+
+
+def spread(enc_kv, copies_of):
+    layers, _, features = enc_kv.shape
+    tiles = enc_kv.reshape(layers, features // HEAD_DIM, HEAD_DIM)
+    return pl.pallas_call(
+        functools.partial(spread_kernel, copies_of),
+        in_specs=[VMEM],
+        out_specs=VMEM,
+        out_shape=jax.ShapeDtypeStruct((layers * copies_of, *tiles.shape[1:]), BF16),
+        compiler_params=pltpu.CompilerParams(vmem_limit_bytes=8 * MIB),
+        name="spread",
+    )(tiles)
+
+
+def project_kernel(states, gain, w_query, w_out, queries, query_mat, out_mat, fresh, gain_buf, sems):
+    fills = (
+        (states.at[pl.ds(0, CAND_LEN), :], fresh),
+        (gain, gain_buf),
+        (w_query, query_mat),
+        (w_out, out_mat),
+    )
+    copies = [pltpu.make_async_copy(*pair, sems.at[i]) for i, pair in enumerate(fills)]
+    for copy in copies:
+        copy.start()
+    copies[0].wait()
+    copies[1].wait()
+    normed = normalize(fresh[...].astype(F32), gain_buf[...]).astype(BF16)
+    copies[2].wait()
+    queries[...] = dot(normed, query_mat[...]).astype(BF16)
+    copies[3].wait()
+
+
+def project(states, gain, mats):
+    width, head_total = mats[0].shape
+    outs = pl.pallas_call(
+        project_kernel,
+        in_specs=[HBM] * 4,
+        out_specs=[VMEM] * 3,
+        out_shape=[
+            jax.ShapeDtypeStruct((CAND_LEN, head_total), BF16),
+            *(pltpu.VMEM(mat.shape, BF16) for mat in mats),
+        ],
+        scratch_shapes=[
+            pltpu.VMEM((CAND_LEN, width), BF16),
+            pltpu.VMEM((1, width), F32),
+            pltpu.SemaphoreType.DMA((4,)),
+        ],
+        compiler_params=pltpu.CompilerParams(vmem_limit_bytes=12 * MIB),
+        cost_estimate=pl.CostEstimate(
+            flops=2 * CAND_LEN * width * head_total,
+            bytes_accessed=4 * width * head_total,
+            transcendentals=0,
+        ),
+        name="project",
+    )(*in_hbm(states, gain, *mats))
+    return outs[0], outs[1:]
+
+
 def attend_kernel(step, capacity, scalars, *refs):
     incoming = states = None
     if step > 0:
         incoming, refs = refs[0], refs[1:]
     if step < CAND_DEV:
         states, refs = refs[0], refs[1:]
-    stream = step == 0
+    if step == 0:
+        projected, refs = refs[0], refs[1:]
     (routes, cached, attn_gain, ffn_gain, router_t, w_query, w_out,
-     after_ref, outgoing, weights), refs = refs[:10], refs[10:]
-    if stream:
-        sources, (w_query, w_out), refs = (w_query, w_out), refs[:2], refs[2:]
-    fresh, gain_buf, router_buf, context, sems = refs
+     after_ref, outgoing, weights,
+     fresh, gain_buf, router_buf, context, sems) = refs
     segment = scalars[0]
     fills = [
         (attn_gain, gain_buf.at[0]),
         (ffn_gain, gain_buf.at[1]),
         (router_t, router_buf),
     ]
-    if stream:
-        fills += [(sources[0], w_query), (sources[1], w_out)]
     if states is not None:
         fills.insert(0, (states.at[pl.ds(step * CAND_LEN, CAND_LEN), :], fresh))
     copies = [pltpu.make_async_copy(*pair, sems.at[i]) for i, pair in enumerate(fills)]
@@ -77,13 +138,14 @@
         current = jnp.where(segment == 0, fresh[...], incoming[...])
     else:
         current = incoming[...]
+    carried = current.astype(F32)
     copies[0].wait()
     copies[1].wait()
-    carried = current.astype(F32)
-    normed = normalize(carried, gain_buf[0]).astype(BF16)
-    if stream:
-        copies[3].wait()
-    queries = dot(normed, w_query[...]).astype(BF16)
+    if step == 0:
+        queries = projected[...]
+    else:
+        normed = normalize(carried, gain_buf[0]).astype(BF16)
+        queries = dot(normed, w_query[...]).astype(BF16)
     head_total = queries.shape[1]
     scale = 1.0 / math.sqrt(HEAD_DIM)
     for start in range(0, head_total, HEAD_DIM):
@@ -93,8 +155,6 @@
         share = (exponent / jnp.sum(exponent, axis=1, keepdims=True)).astype(BF16)
         values = cached[:, head_total + start : head_total + start + HEAD_DIM]
         context[:, lanes] = dot(share, values).astype(BF16)
-    if stream:
-        copies[4].wait()
     after_attn = carried + dot(context[...], w_out[...])
     after_ref[...] = after_attn
     ffn_input = normalize(after_attn, gain_buf[1]).astype(BF16)
@@ -127,11 +187,10 @@
     weights[...] = jnp.where(chosen[0], gate_first, 0.0) + jnp.where(chosen[1], gate_second, 0.0)
 
 
-def attend(step, capacity, scalars, states, incoming, routes, cached, gains, router_t, mats):
+def attend(step, capacity, scalars, states, incoming, queries, routes, cached, gains, router_t, mats):
     w_query, w_out = mats
-    width, head_total = w_query.shape
+    head_total, width = w_out.shape
     slot_count = router_t.shape[0] * capacity
-    stream = step == 0
     sources, specs = [], []
     if step > 0:
         sources.append(incoming)
@@ -139,24 +198,24 @@
     if step < CAND_DEV:
         sources += in_hbm(states)
         specs.append(HBM)
-    out_shape = [
-        jax.ShapeDtypeStruct((CAND_LEN, width), F32),
-        jax.ShapeDtypeStruct((slot_count, width), BF16),
-        jax.ShapeDtypeStruct((CAND_LEN, slot_count), F32),
-    ]
-    if stream:
-        out_shape += [pltpu.VMEM(mat.shape, BF16) for mat in mats]
-    outs = pl.pallas_call(
+    if step == 0:
+        sources.append(queries)
+        specs.append(VMEM)
+    return pl.pallas_call(
         functools.partial(attend_kernel, step, capacity),
-        in_specs=[SMEM] + specs + [VMEM, VMEM, HBM, HBM, HBM] + [HBM if stream else VMEM] * 2,
-        out_specs=[VMEM] * len(out_shape),
-        out_shape=out_shape,
+        in_specs=[SMEM] + specs + [VMEM, VMEM, HBM, HBM, HBM, VMEM, VMEM],
+        out_specs=[VMEM] * 3,
+        out_shape=[
+            jax.ShapeDtypeStruct((CAND_LEN, width), F32),
+            jax.ShapeDtypeStruct((slot_count, width), BF16),
+            jax.ShapeDtypeStruct((CAND_LEN, slot_count), F32),
+        ],
         scratch_shapes=[
             pltpu.VMEM((CAND_LEN, width), BF16),
             pltpu.VMEM((2, 1, width), F32),
             pltpu.VMEM(router_t.shape, BF16),
             pltpu.VMEM((CAND_LEN, head_total), BF16),
-            pltpu.SemaphoreType.DMA((6,)),
+            pltpu.SemaphoreType.DMA((4,)),
         ],
         compiler_params=pltpu.CompilerParams(vmem_limit_bytes=12 * MIB),
         cost_estimate=pl.CostEstimate(
@@ -166,10 +225,8 @@
         ),
         name="attend",
     )(
-        scalars, *sources, routes, cached, *in_hbm(*gains, router_t),
-        *(in_hbm(*mats) if stream else in_vmem(*mats)),
+        scalars, *sources, routes, cached, *in_hbm(*gains, router_t), *in_vmem(w_query, w_out)
     )
-    return outs[:3], (outs[3:] if stream else mats)
 
 
 def expert_kernel(stream, rows, *refs):
@@ -288,8 +345,8 @@
     scratch = []
     out_shape, out_spec = jax.ShapeDtypeStruct((rows, width), BF16), VMEM
     if earlier:
-        inputs += [scalars, *in_hbm(*earlier)]
-        specs += [SMEM] + [HBM] * len(earlier)
+        inputs += [scalars, *in_vmem(*earlier)]
+        specs += [SMEM] + [VMEM] * len(earlier)
         scratch = [pltpu.VMEM((rows, width), BF16), pltpu.SemaphoreType.DMA((CAND_DEV,))]
         out_shape, out_spec = jax.ShapeDtypeStruct((CAND_DEV * rows, width), BF16), HBM
     return pl.pallas_call(
@@ -327,24 +384,24 @@
         )
         return moved.reshape(rows.shape)
 
-    spread = jnp.repeat(enc_kv[:, 0, :], n_expert, axis=0)
     cached = lax.all_to_all(
-        spread, ("segment", "expert"), split_axis=0, concat_axis=0, tiled=True
+        spread(enc_kv, n_expert), ("segment", "expert"), split_axis=0, concat_axis=0, tiled=True
     )
+    cached = cached.reshape(cached.shape[0], -1)
     own = (w_in[0, 0], w_down[0, 0])
     other = tuple(lax.ppermute(mat, "expert", core_pairs) for mat in own)
 
     scalars = jnp.concatenate([segment_index.astype(jnp.int32).reshape(1), cand_len])
     route_all = routes[0].reshape(CAND_DEV, CAND_LEN, 2)
     router_t = w_router[0].T
-    attend_mats = (w_query[0], w_out[0])
+    queries, attend_mats = project(states, attn_gain, (w_query[0], w_out[0]))
     expert_mats = (*own, *other)
     step_count = CAND_DEV + n_segment - 1
     incoming = None
     earlier = []
     for step in range(step_count):
-        (after_attn, outgoing, weights), attend_mats = attend(
-            step, capacity, scalars, states, incoming, route_all, cached,
+        after_attn, outgoing, weights = attend(
+            step, capacity, scalars, states, incoming, queries, route_all, cached,
             (attn_gain, ffn_gain), router_t, attend_mats,
         )
         served, expert_mats = expert_rows(exchange(outgoing), expert_mats, step == 0)

time: 243 us -> 229 us (0.942)
  Pallas kernels: 83.4 us -> 69.4 us
  waiting for transfers between devices: 22.1 us -> 15.4 us
  local copies, waits for them, and re-layouts: 5.83 us -> 9.85 us
    pallas_call x5, Pallas kernels: 18.9 us -> 2.72 us  [combine(): pl.pallas_call(place_kernel if earlier else combine_kernel, in_specs=spec...]
    all_to_all x1, waiting for transfers between devices: 6.71 us -> 0.01 us  [local(): lax.all_to_all(spread(enc_kv, n_expert), ('segment', 'expert'), split_axi...]
    unnamed x20 -> x17, local copies, waits for them, and re-layouts: 5.3 us -> 9.85 us
    pallas_call x0 -> x2, Pallas kernels: none -> 4.27 us  [the longest x1 3.6 us: project(): pl.pallas_call(project_kernel, in_specs=[HBM] * 4, out_specs=[VMEM] * 3,...]
  transfers between devices with their start and end apart: 7 -> 7, of which waited for: 5 -> 4; matrix products, arithmetic and copies ran while one was open for 2% -> 1% of each run, Pallas kernels for 3% -> 4%
where the time goes in v4:
time: 229 us
  blocking collectives  109 us (48%)
  Pallas kernels  69.4 us (30%)
  starting transfers between devices  24.4 us (11%)
  waiting for transfers between devices  15.4 us (7%)
  local copies, waits for them, and re-layouts  9.85 us (4%)
    all_to_all x10, blocking collectives, exchange(): lax.all_to_all(blocks, 'expert', split_axis=0, concat_axis=0, axis_index_...  109 us
    pallas_call x5, Pallas kernels, expert_rows(): pl.pallas_call(functools.partial(expert_kernel, stream), in_specs=[VMEM]...  40.1 us
    pallas_call x5, Pallas kernels, attend(): pl.pallas_call(functools.partial(attend_kernel, step, capacity), in_specs...  22.2 us
    ppermute x4, starting transfers between devices, local(): lax.ppermute(result, 'segment', [(i, i + 1) for i in range(n_segment - 1)])  16.6 us
    ppermute x4, waiting for transfers between devices, local(): lax.ppermute(result, 'segment', [(i, i + 1) for i in range(n_segment - 1)])  15.4 us
    unnamed x17, local copies, waits for them, and re-layouts  9.85 us
    all_to_all x1, starting transfers between devices, local(): lax.all_to_all(spread(enc_kv, n_expert), ('segment', 'expert'), split_axi...  7.29 us
  transfers between devices with their start and end apart: 7, of which 4 were waited for; matrix products, arithmetic and copies ran while one was open for 1% of the time, Pallas kernels for 4%

profile of v4, /device:TPU:0, one launch (start us, length us, event | category | flops | bytes accessed | tf_op | source)
XLA Modules:
  0.0 228.6 jit_solution(13674304534656931324)
XLA Ops:
  1.9 7.3 %all-to-all-start = ((bf16[32,16,128]{2,1,0:T(8,128)(2,1)}), bf16[32,16,128]{2,1,0:T(8,128)(2,1)S(1)}, u32[]{:S(2)}, u32[]{:S(2)}) async-start(bf16[32,16,128]{2,1,0:T(8,128)(2,1)} %spread.1), calls=%async_computation | async-start | bytes 262144 | tf_op jit(solution)/shard_map/all_to_all | solution.py:387
  10.0 3.6 %project.1 = (bf16[64,1024]{1,0:T(8,128)(2,1)S(1)}, bf16[2048,1024]{1,0:T(8,128)(2,1)S(1)}, bf16[1024,2048]{1,0:T(8,128)(2,1)S(1)}) custom-call(bf16[128,2048]{1,0:T(8,128)(2,1)} %refs_1_.1, f32[1,2048]{1,0:T(1,128)} %refs_3_.5, bf16[2048,1024]{1,0:T(8,128)(2,1)} %bitcast.75, bf16[1024,2048]{1,0:T(8,128)(2,1)} %bitcast.76), custom_call_target="tpu_custom_call" | custom-call | flops 268435456 | bytes 8388608 | tf_op jit(solution)/shard_map/project/pallas_call | solution.py:85
  17.7 2.2 copy-done.1
  19.9 2.2 copy-done.4
  22.0 4.1 %attend.5 = (f32[64,2048]{1,0:T(8,128)S(1)}, bf16[160,2048]{1,0:T(8,128)(2,1)S(1)}, f32[64,160]{1,0:T(8,128)S(1)}) custom-call(s32[3]{0:T(128)S(1)} %pad_add_fusion.scalars, bf16[128,2048]{1,0:T(8,128)(2,1)} %refs_1_.1, bf16[64,1024]{1,0:T(8,128)(2,1)S(1)} %get-tuple-element.28.refs_1_, s32[2,64,2]{2,1,0:T(8,128)S(1)} %bitcast.59, ...), custom_call_target="tpu_custom_call" | custom-call | flops 805306368 | bytes 9437184 | tf_op jit(solution)/shard_map/attend/pallas_call | solution.py:204
  26.1 14.0 %all_to_all.55 = bf16[4,40,2048]{2,1,0:T(8,128)(2,1)S(1)} all-to-all(bf16[4,40,2048]{2,1,0:T(8,128)(2,1)S(1)} %bitcast.66), channel_id=1, replica_groups={{0,2,4,6},{1,3,5,7},{8,10,12,14},{9,11,13,15},{16,18,20,22},{17,19,21,2..., dimensions={0} | all-to-all | bytes 1310720 | tf_op jit(solution)/shard_map/all_to_all | solution.py:382
  40.1 12.1 %experts.5 = (bf16[160,2048]{1,0:T(8,128)(2,1)S(1)}, bf16[2048,2048]{1,0:T(8,128)(2,1)S(1)}, bf16[2048,2048]{1,0:T(8,128)(2,1)S(1)}, bf16[2048,2048]{1,0:T(8,128)(2,1)S(1)}, bf16[2048,2048]{1,0:T(8,128)(2,1)S(1)}) custom-call(bf16[160,2048]{1,0:T(8,128)(2,1)S(1)} %bitcast.50, bf16[2048,2048]{1,0:T(8,128)(2,1)} %bitcast.72, bf16[2048,2048]{1,0:T(8,128)(2,1)} %bitcast.74, ...), custom_call_target="tpu_custom_call" | custom-call | flops 5368709120 | bytes 34865152 | tf_op jit(solution)/shard_map/experts/pallas_call | solution.py:285
  52.2 11.3 %all_to_all.56 = bf16[4,40,2048]{2,1,0:T(8,128)(2,1)S(1)} all-to-all(bf16[4,40,2048]{2,1,0:T(8,128)(2,1)S(1)} %bitcast.64), channel_id=1, replica_groups={{0,2,4,6},{1,3,5,7},{8,10,12,14},{9,11,13,15},{16,18,20,22},{17,19,21,2..., dimensions={0} | all-to-all | bytes 1310720 | tf_op jit(solution)/shard_map/all_to_all | solution.py:382
  63.9 3.4 %collective-permute-start.2 = (bf16[64,2048]{1,0:T(8,128)(2,1)S(1)}, bf16[64,2048]{1,0:T(8,128)(2,1)S(1)}, u32[]{:S(2)}, u32[]{:S(2)}) collective-permute-start(bf16[64,2048]{1,0:T(8,128)(2,1)S(1)} %combine.5.refs_0_), channel_id=1, source_target_pairs={{0,8},{8,16},{16,24},{1,9},{9,17},{17,25},{2,10},{10,18},{18,26},{... | collective-permute-start | bytes 786440 | tf_op jit(solution)/shard_map/ppermute | solution.py:411
  67.3 3.9 %collective-permute-done.2.refs_0_ = bf16[64,2048]{1,0:T(8,128)(2,1)S(1)} collective-permute-done((bf16[64,2048]{1,0:T(8,128)(2,1)S(1)}, bf16[64,2048]{1,0:T(8,128)(2,1)S(1)}, u32[]{:S(2)}, u32[]{:S(2)}) %collective-permute-start.2) | collective-permute-done | bytes 262176 | tf_op jit(solution)/shard_map/ppermute | solution.py:411
  71.1 4.8 %attend.6 = (f32[64,2048]{1,0:T(8,128)S(1)}, bf16[160,2048]{1,0:T(8,128)(2,1)S(1)}, f32[64,160]{1,0:T(8,128)S(1)}) custom-call(s32[3]{0:T(128)S(1)} %pad_add_fusion.scalars, bf16[64,2048]{1,0:T(8,128)(2,1)S(1)} %collective-permute-done.2.refs_0_, bf16[128,2048]{1,0:T(8,128)(2,1)} %refs_1_.1, s32[2,64,2]{2,1,0:T(8,128)S(1)} %bitcast.60, ...), custom_call_target="tpu_custom_call" | custom-call | flops 805306368 | bytes 9437184 | tf_op jit(solution)/shard_map/attend/pallas_call | solution.py:204
  75.9 10.2 %all_to_all.57 = bf16[4,40,2048]{2,1,0:T(8,128)(2,1)S(1)} all-to-all(bf16[4,40,2048]{2,1,0:T(8,128)(2,1)S(1)} %bitcast.67), channel_id=1, replica_groups={{0,2,4,6},{1,3,5,7},{8,10,12,14},{9,11,13,15},{16,18,20,22},{17,19,21,2..., dimensions={0} | all-to-all | bytes 1310720 | tf_op jit(solution)/shard_map/all_to_all | solution.py:382
  86.1 7.0 %experts.6 = bf16[160,2048]{1,0:T(8,128)(2,1)S(1)} custom-call(bf16[160,2048]{1,0:T(8,128)(2,1)S(1)} %bitcast.53, bf16[2048,2048]{1,0:T(8,128)(2,1)S(1)} %get-tuple-element.38.refs_0_, bf16[2048,2048]{1,0:T(8,128)(2,1)S(1)} %get-tuple-element.39.refs_1_, bf16[2048,2048]{1,0:T(8,128)(2,1)S(1)} %get-tuple-element.40.refs_2_, ...), custom_call_target="tpu_custom_call" | custom-call | flops 5368709120 | bytes 34865152 | tf_op jit(solution)/shard_map/experts/pallas_call | solution.py:285
  93.2 10.2 %all_to_all.58 = bf16[4,40,2048]{2,1,0:T(8,128)(2,1)S(1)} all-to-all(bf16[4,40,2048]{2,1,0:T(8,128)(2,1)S(1)} %bitcast.54), channel_id=1, replica_groups={{0,2,4,6},{1,3,5,7},{8,10,12,14},{9,11,13,15},{16,18,20,22},{17,19,21,2..., dimensions={0} | all-to-all | bytes 1310720 | tf_op jit(solution)/shard_map/all_to_all | solution.py:382
  103.8 4.4 %collective-permute-start.3 = (bf16[64,2048]{1,0:T(8,128)(2,1)S(1)}, bf16[64,2048]{1,0:T(8,128)(2,1)S(1)}, u32[]{:S(2)}, u32[]{:S(2)}) collective-permute-start(bf16[64,2048]{1,0:T(8,128)(2,1)S(1)} %combine.6.refs_1_), channel_id=1, source_target_pairs={{0,8},{8,16},{16,24},{1,9},{9,17},{17,25},{2,10},{10,18},{18,26},{... | collective-permute-start | bytes 786440 | tf_op jit(solution)/shard_map/ppermute | solution.py:411
  108.2 3.9 %collective-permute-done.3.refs_0_ = bf16[64,2048]{1,0:T(8,128)(2,1)S(1)} collective-permute-done((bf16[64,2048]{1,0:T(8,128)(2,1)S(1)}, bf16[64,2048]{1,0:T(8,128)(2,1)S(1)}, u32[]{:S(2)}, u32[]{:S(2)}) %collective-permute-start.3) | collective-permute-done | bytes 262176 | tf_op jit(solution)/shard_map/ppermute | solution.py:411
  112.0 4.5 %attend.7 = (f32[64,2048]{1,0:T(8,128)S(1)}, bf16[160,2048]{1,0:T(8,128)(2,1)S(1)}, f32[64,160]{1,0:T(8,128)S(1)}) custom-call(s32[3]{0:T(128)S(1)} %pad_add_fusion.scalars, bf16[64,2048]{1,0:T(8,128)(2,1)S(1)} %collective-permute-done.3.refs_0_, s32[2,64,2]{2,1,0:T(8,128)S(1)} %bitcast.61, bf16[32,2048]{1,0:T(8,128)(2,1)S(1)} %bitcast.42, ...), custom_call_target="tpu_custom_call" | custom-call | flops 805306368 | bytes 9437184 | tf_op jit(solution)/shard_map/attend/pallas_call | solution.py:204
  116.5 10.2 %all_to_all.59 = bf16[4,40,2048]{2,1,0:T(8,128)(2,1)S(1)} all-to-all(bf16[4,40,2048]{2,1,0:T(8,128)(2,1)S(1)} %bitcast.68), channel_id=1, replica_groups={{0,2,4,6},{1,3,5,7},{8,10,12,14},{9,11,13,15},{16,18,20,22},{17,19,21,2..., dimensions={0} | all-to-all | bytes 1310720 | tf_op jit(solution)/shard_map/all_to_all | solution.py:382
  126.7 7.0 %experts.7 = bf16[160,2048]{1,0:T(8,128)(2,1)S(1)} custom-call(bf16[160,2048]{1,0:T(8,128)(2,1)S(1)} %bitcast.55, bf16[2048,2048]{1,0:T(8,128)(2,1)S(1)} %get-tuple-element.38.refs_0_, bf16[2048,2048]{1,0:T(8,128)(2,1)S(1)} %get-tuple-element.39.refs_1_, bf16[2048,2048]{1,0:T(8,128)(2,1)S(1)} %get-tuple-element.40.refs_2_, ...), custom_call_target="tpu_custom_call" | custom-call | flops 5368709120 | bytes 34865152 | tf_op jit(solution)/shard_map/experts/pallas_call | solution.py:285
  133.8 10.2 %all_to_all.60 = bf16[4,40,2048]{2,1,0:T(8,128)(2,1)S(1)} all-to-all(bf16[4,40,2048]{2,1,0:T(8,128)(2,1)S(1)} %bitcast.56), channel_id=1, replica_groups={{0,2,4,6},{1,3,5,7},{8,10,12,14},{9,11,13,15},{16,18,20,22},{17,19,21,2..., dimensions={0} | all-to-all | bytes 1310720 | tf_op jit(solution)/shard_map/all_to_all | solution.py:382
  144.4 4.4 %collective-permute-start.4 = (bf16[64,2048]{1,0:T(8,128)(2,1)S(1)}, bf16[64,2048]{1,0:T(8,128)(2,1)S(1)}, u32[]{:S(2)}, u32[]{:S(2)}) collective-permute-start(bf16[64,2048]{1,0:T(8,128)(2,1)S(1)} %combine.7.refs_2_), channel_id=1, source_target_pairs={{0,8},{8,16},{16,24},{1,9},{9,17},{17,25},{2,10},{10,18},{18,26},{... | collective-permute-start | bytes 786440 | tf_op jit(solution)/shard_map/ppermute | solution.py:411
  148.8 3.9 %collective-permute-done.4.refs_0_ = bf16[64,2048]{1,0:T(8,128)(2,1)S(1)} collective-permute-done((bf16[64,2048]{1,0:T(8,128)(2,1)S(1)}, bf16[64,2048]{1,0:T(8,128)(2,1)S(1)}, u32[]{:S(2)}, u32[]{:S(2)}) %collective-permute-start.4) | collective-permute-done | bytes 262176 | tf_op jit(solution)/shard_map/ppermute | solution.py:411
  152.6 4.5 %attend.8 = (f32[64,2048]{1,0:T(8,128)S(1)}, bf16[160,2048]{1,0:T(8,128)(2,1)S(1)}, f32[64,160]{1,0:T(8,128)S(1)}) custom-call(s32[3]{0:T(128)S(1)} %pad_add_fusion.scalars, bf16[64,2048]{1,0:T(8,128)(2,1)S(1)} %collective-permute-done.4.refs_0_, s32[2,64,2]{2,1,0:T(8,128)S(1)} %bitcast.62, bf16[32,2048]{1,0:T(8,128)(2,1)S(1)} %bitcast.43, ...), custom_call_target="tpu_custom_call" | custom-call | flops 805306368 | bytes 9437184 | tf_op jit(solution)/shard_map/attend/pallas_call | solution.py:204
  157.1 10.2 %all_to_all.61 = bf16[4,40,2048]{2,1,0:T(8,128)(2,1)S(1)} all-to-all(bf16[4,40,2048]{2,1,0:T(8,128)(2,1)S(1)} %bitcast.69), channel_id=1, replica_groups={{0,2,4,6},{1,3,5,7},{8,10,12,14},{9,11,13,15},{16,18,20,22},{17,19,21,2..., dimensions={0} | all-to-all | bytes 1310720 | tf_op jit(solution)/shard_map/all_to_all | solution.py:382
  167.3 7.0 %experts.8 = bf16[160,2048]{1,0:T(8,128)(2,1)S(1)} custom-call(bf16[160,2048]{1,0:T(8,128)(2,1)S(1)} %bitcast.57, bf16[2048,2048]{1,0:T(8,128)(2,1)S(1)} %get-tuple-element.38.refs_0_, bf16[2048,2048]{1,0:T(8,128)(2,1)S(1)} %get-tuple-element.39.refs_1_, bf16[2048,2048]{1,0:T(8,128)(2,1)S(1)} %get-tuple-element.40.refs_2_, ...), custom_call_target="tpu_custom_call" | custom-call | flops 5368709120 | bytes 34865152 | tf_op jit(solution)/shard_map/experts/pallas_call | solution.py:285
  174.4 10.2 %all_to_all.62 = bf16[4,40,2048]{2,1,0:T(8,128)(2,1)S(1)} all-to-all(bf16[4,40,2048]{2,1,0:T(8,128)(2,1)S(1)} %bitcast.58), channel_id=1, replica_groups={{0,2,4,6},{1,3,5,7},{8,10,12,14},{9,11,13,15},{16,18,20,22},{17,19,21,2..., dimensions={0} | all-to-all | bytes 1310720 | tf_op jit(solution)/shard_map/all_to_all | solution.py:382
  185.0 4.4 %collective-permute-start.5 = (bf16[64,2048]{1,0:T(8,128)(2,1)S(1)}, bf16[64,2048]{1,0:T(8,128)(2,1)S(1)}, u32[]{:S(2)}, u32[]{:S(2)}) collective-permute-start(bf16[64,2048]{1,0:T(8,128)(2,1)S(1)} %combine.8.refs_3_), channel_id=1, source_target_pairs={{0,8},{8,16},{16,24},{1,9},{9,17},{17,25},{2,10},{10,18},{18,26},{... | collective-permute-start | bytes 786440 | tf_op jit(solution)/shard_map/ppermute | solution.py:411
  189.4 3.9 %collective-permute-done.5.refs_0_ = bf16[64,2048]{1,0:T(8,128)(2,1)S(1)} collective-permute-done((bf16[64,2048]{1,0:T(8,128)(2,1)S(1)}, bf16[64,2048]{1,0:T(8,128)(2,1)S(1)}, u32[]{:S(2)}, u32[]{:S(2)}) %collective-permute-start.5) | collective-permute-done | bytes 262176 | tf_op jit(solution)/shard_map/ppermute | solution.py:411
  193.2 4.5 %attend.9 = (f32[64,2048]{1,0:T(8,128)S(1)}, bf16[160,2048]{1,0:T(8,128)(2,1)S(1)}, f32[64,160]{1,0:T(8,128)S(1)}) custom-call(s32[3]{0:T(128)S(1)} %pad_add_fusion.scalars, bf16[64,2048]{1,0:T(8,128)(2,1)S(1)} %collective-permute-done.5.refs_0_, s32[2,64,2]{2,1,0:T(8,128)S(1)} %bitcast.63, bf16[32,2048]{1,0:T(8,128)(2,1)S(1)} %bitcast.44, ...), custom_call_target="tpu_custom_call" | custom-call | flops 805306368 | bytes 9437184 | tf_op jit(solution)/shard_map/attend/pallas_call | solution.py:204
  197.7 12.1 %all_to_all.63 = bf16[4,40,2048]{2,1,0:T(8,128)(2,1)S(1)} all-to-all(bf16[4,40,2048]{2,1,0:T(8,128)(2,1)S(1)} %bitcast.65), channel_id=1, replica_groups={{0,2,4,6},{1,3,5,7},{8,10,12,14},{9,11,13,15},{16,18,20,22},{17,19,21,2..., dimensions={0} | all-to-all | bytes 1310720 | tf_op jit(solution)/shard_map/all_to_all | solution.py:382
  209.8 7.0 %experts.9 = bf16[160,2048]{1,0:T(8,128)(2,1)S(1)} custom-call(bf16[160,2048]{1,0:T(8,128)(2,1)S(1)} %bitcast.51, bf16[2048,2048]{1,0:T(8,128)(2,1)S(1)} %get-tuple-element.38.refs_0_, bf16[2048,2048]{1,0:T(8,128)(2,1)S(1)} %get-tuple-element.39.refs_1_, bf16[2048,2048]{1,0:T(8,128)(2,1)S(1)} %get-tuple-element.40.refs_2_, ...), custom_call_target="tpu_custom_call" | custom-call | flops 5368709120 | bytes 34865152 | tf_op jit(solution)/shard_map/experts/pallas_call | solution.py:285
  216.8 10.2 %all_to_all.64 = bf16[4,40,2048]{2,1,0:T(8,128)(2,1)S(1)} all-to-all(bf16[4,40,2048]{2,1,0:T(8,128)(2,1)S(1)} %bitcast.52), channel_id=1, replica_groups={{0,2,4,6},{1,3,5,7},{8,10,12,14},{9,11,13,15},{16,18,20,22},{17,19,21,2..., dimensions={0} | all-to-all | bytes 1310720 | tf_op jit(solution)/shard_map/all_to_all | solution.py:382
  (27 shorter events, 9.5 us)
Async XLA Ops:
  0.0 17.5 %copy-start.6 = (s32[2]{0:T(128)S(1)}, s32[2]{0:T(128)}, u32[]{:S(2)}) copy-start(s32[2]{0:T(128)} %param.12) | copy-start | bytes 28
  0.0 40.1 %collective-permute-start = (bf16[2048,2048]{1,0:T(8,128)(2,1)}, bf16[2048,2048]{1,0:T(8,128)(2,1)}, u32[]{:S(2)}, u32[]{:S(2)}) collective-permute-start(bf16[2048,2048]{1,0:T(8,128)(2,1)} %bitcast.71), channel_id=1, source_target_pairs={{0,1},{1,0},{2,3},{3,2},{4,5},{5,4},{6,7},{7,6},{8,9},{9,8},{10,11... | collective-permute-start | bytes 25165832 | tf_op jit(solution)/shard_map/ppermute | solution.py:392
  0.5 39.6 %collective-permute-start.1 = (bf16[2048,2048]{1,0:T(8,128)(2,1)}, bf16[2048,2048]{1,0:T(8,128)(2,1)}, u32[]{:S(2)}, u32[]{:S(2)}) collective-permute-start(bf16[2048,2048]{1,0:T(8,128)(2,1)} %bitcast.73), channel_id=1, source_target_pairs={{0,1},{1,0},{2,3},{3,2},{4,5},{5,4},{6,7},{7,6},{8,9},{9,8},{10,11... | collective-permute-start | bytes 25165832 | tf_op jit(solution)/shard_map/ppermute | solution.py:392
  1.9 15.7 %all-to-all-start = ((bf16[32,16,128]{2,1,0:T(8,128)(2,1)}), bf16[32,16,128]{2,1,0:T(8,128)(2,1)S(1)}, u32[]{:S(2)}, u32[]{:S(2)}) async-start(bf16[32,16,128]{2,1,0:T(8,128)(2,1)} %spread.1), calls=%async_computation | async-start | bytes 262144 | tf_op jit(solution)/shard_map/all_to_all | solution.py:387
  13.6 1.9 copy-start
  15.6 2.0 copy-start.3
  17.7 2.2 copy-start.1
  19.9 2.2 copy-start.4
  40.1 31.0 %copy-start.2 = (bf16[2048,1024]{1,0:T(8,128)(2,1)S(1)}, bf16[2048,1024]{1,0:T(8,128)(2,1)}, u32[]{:S(2)}) copy-start(bf16[2048,1024]{1,0:T(8,128)(2,1)} %copy-done) | copy-start | bytes 12582916
  40.1 31.0 %copy-start.5 = (bf16[1024,2048]{1,0:T(8,128)(2,1)S(1)}, bf16[1024,2048]{1,0:T(8,128)(2,1)}, u32[]{:S(2)}) copy-start(bf16[1024,2048]{1,0:T(8,128)(2,1)} %copy-done.3) | copy-start | bytes 12582916
  63.9 7.3 %collective-permute-start.2 = (bf16[64,2048]{1,0:T(8,128)(2,1)S(1)}, bf16[64,2048]{1,0:T(8,128)(2,1)S(1)}, u32[]{:S(2)}, u32[]{:S(2)}) collective-permute-start(bf16[64,2048]{1,0:T(8,128)(2,1)S(1)} %combine.5.refs_0_), channel_id=1, source_target_pairs={{0,8},{8,16},{16,24},{1,9},{9,17},{17,25},{2,10},{10,18},{18,26},{... | collective-permute-start | bytes 786440 | tf_op jit(solution)/shard_map/ppermute | solution.py:411
  103.8 8.3 %collective-permute-start.3 = (bf16[64,2048]{1,0:T(8,128)(2,1)S(1)}, bf16[64,2048]{1,0:T(8,128)(2,1)S(1)}, u32[]{:S(2)}, u32[]{:S(2)}) collective-permute-start(bf16[64,2048]{1,0:T(8,128)(2,1)S(1)} %combine.6.refs_1_), channel_id=1, source_target_pairs={{0,8},{8,16},{16,24},{1,9},{9,17},{17,25},{2,10},{10,18},{18,26},{... | collective-permute-start | bytes 786440 | tf_op jit(solution)/shard_map/ppermute | solution.py:411
  144.4 8.3 %collective-permute-start.4 = (bf16[64,2048]{1,0:T(8,128)(2,1)S(1)}, bf16[64,2048]{1,0:T(8,128)(2,1)S(1)}, u32[]{:S(2)}, u32[]{:S(2)}) collective-permute-start(bf16[64,2048]{1,0:T(8,128)(2,1)S(1)} %combine.7.refs_2_), channel_id=1, source_target_pairs={{0,8},{8,16},{16,24},{1,9},{9,17},{17,25},{2,10},{10,18},{18,26},{... | collective-permute-start | bytes 786440 | tf_op jit(solution)/shard_map/ppermute | solution.py:411
  185.0 8.3 %collective-permute-start.5 = (bf16[64,2048]{1,0:T(8,128)(2,1)S(1)}, bf16[64,2048]{1,0:T(8,128)(2,1)S(1)}, u32[]{:S(2)}, u32[]{:S(2)}) collective-permute-start(bf16[64,2048]{1,0:T(8,128)(2,1)S(1)} %combine.8.refs_3_), channel_id=1, source_target_pairs={{0,8},{8,16},{16,24},{1,9},{9,17},{17,25},{2,10},{10,18},{18,26},{... | collective-permute-start | bytes 786440 | tf_op jit(solution)/shard_map/ppermute | solution.py:411
